TPU v7x, 512 devices: a whole 4x8x8 slice. The times are simulated.
512 devices in a mesh: seq: 32 (over y, x), vocab: 16 (over z, core).
Axes of the slice: x: 4, y: 8, z: 8, core: 2. Of those that a mesh axis runs over, the one named last changes fastest.
Arguments:
- queries: bfloat16 [16384, 4096], P('seq', 'vocab'), may hold values from -220 to 220
- keys: bfloat16 [16384, 512], P('seq'), may hold values from -6 to 6
- values: bfloat16 [16384, 512], P('seq'), may hold values from -6 to 6
- sinks: float32 [64], P('vocab'), may hold values from 0 to 3
- doc_ids: int32 [16384], P('seq'), may hold values from 0 to 63, never falling along the last dimension, each value on 1 to 512 neighbouring positions
- upper_grad: bfloat16 [16384, 4096], P('seq', 'vocab'), may hold values from -6 to 6
- out_proj: bfloat16 [4096, 2880], P('vocab'), may hold values from -0.09375 to 0.09375
- final_hidden: bfloat16 [256, 2880], P('seq'), may hold values from -70 to 70
- advantages: bfloat16 [256], P('seq'), may hold values from -4 to 4
- slot_pos: int32 [256], P('seq'), may hold values from 0 to 511, as said below
- slot_live: int32 [256], P('seq'), may hold values 0 or 1
- sampled_ids: int32 [256], P('seq'), may hold values from 0 to 102399
- policy_head: bfloat16 [102400, 2880], P(('seq', 'vocab')), may hold values from -0.109375 to 0.109375
- reference_head: bfloat16 [102400, 2880], P(('seq', 'vocab')), may hold values from -0.109375 to 0.109375
Outputs:
- grad_queries: bfloat16 [16384, 4096], P('seq', 'vocab')
- grad_kv: bfloat16 [2, 512, 16384], P(None, 'vocab', 'seq')
- grad_sinks: float32 [64], P('vocab')
- hidden_grad: float32 [256, 2880], P('seq')
Inputs may be any that keep to these rules, and one draw needn't show every extreme that they name: `slot_pos`: within one owner's 8 slots the positions are distinct.
All inputs are finite; a program needn't handle non-finite values. No bound on the sum of `slot_live` on one device may be relied on, other than what follows from the above.
Results may differ from a plain program's by a relative error of at most 0.022.
Values may be sent and summed in bfloat16 or wider, within the bound.
A program may use at most 64 MiB of HBM per device.

v0:
```python
import jax
import jax.numpy as jnp
from jax import lax
from jax.sharding import PartitionSpec as P

HD = 64
WINDOW = 128


loss_scale = 64.0
kl_weight = 1.0
masked_score = -1e30
contract_last = (((1,), (1,)), ((), ()))
contract_first = (((0,), (0,)), ((), ()))


def passed_along(value, axis, steps):
    count = lax.axis_size(axis)
    leading, last = (max(0, -steps), min(count, count - steps))
    return lax.ppermute(value, axis, [(source, source + steps) for source in range(leading, last)])


def partner(shard, axis, distance):
    return lax.ppermute(shard, axis, [(i, i ^ 1 << distance) for i in range(lax.axis_size(axis))])


def strip_rows(extended, tiles, window):
    shaped = extended.reshape((tiles + 1, window) + extended.shape[1:])
    return jnp.concatenate([shaped[:-1], shaped[1:]], axis=1)


def shards(
    queries,
    keys,
    values,
    sinks,
    doc_ids,
    upper_grad,
    out_proj,
    final_hidden,
    advantages,
    slot_pos,
    slot_live,
    sampled_ids,
    policy_head,
    reference_head,
):
    rows_hidden, rows_advantage = (
        lax.all_gather(final_hidden, "seq", axis=0, tiled=True),
        lax.all_gather(advantages, "seq", axis=0, tiled=True),
    )
    rows_ids, rows_live = (
        lax.all_gather(sampled_ids, "seq", axis=0, tiled=True),
        lax.all_gather(slot_live, "seq", axis=0, tiled=True),
    )
    policy_logits = lax.dot_general(
        policy_head, rows_hidden, contract_last, preferred_element_type=jnp.float32
    )
    frozen_logits = lax.dot_general(
        reference_head, rows_hidden, contract_last, preferred_element_type=jnp.float32
    )
    policy_peak = jnp.max(policy_logits, axis=0)
    frozen_peak = jnp.max(frozen_logits, axis=0)
    logit_diff = policy_logits - frozen_logits
    top_policy, top_frozen = lax.pmax((policy_peak, frozen_peak), ("seq", "vocab"))
    policy_terms = jnp.exp(policy_logits - top_policy)
    local_mass = jnp.sum(policy_terms, axis=0)
    local_cross = jnp.sum(policy_terms * logit_diff, axis=0)
    local_frozen = jnp.sum(jnp.exp(frozen_logits - top_frozen), axis=0)
    total_mass, total_cross, total_frozen = lax.psum(
        (local_mass, local_cross, local_frozen), ("seq", "vocab")
    )
    policy_lognorm = top_policy + jnp.log(total_mass)
    frozen_lognorm = top_frozen + jnp.log(total_frozen)
    policy_prob = jnp.exp(policy_logits - policy_lognorm)
    cross_total = total_cross / total_mass
    divergence = cross_total - policy_lognorm + frozen_lognorm
    first_id = lax.axis_index(("seq", "vocab")) * policy_head.shape[0]
    ids_here = first_id + lax.broadcasted_iota(jnp.int32, policy_logits.shape, 0)
    picked = (ids_here == rows_ids[None, :]).astype(jnp.float32)
    weight = loss_scale * rows_live.astype(jnp.float32)
    advantage_rows = rows_advantage.astype(jnp.float32)
    log_ratio = policy_logits - policy_lognorm - (frozen_logits - frozen_lognorm) - divergence
    logit_grad = (
        weight * (-advantage_rows * (picked - policy_prob) + kl_weight * policy_prob * log_ratio)
    ).astype(jnp.bfloat16)
    owned_rows = lax.psum_scatter(
        lax.dot_general(
            logit_grad, policy_head, contract_first, preferred_element_type=jnp.float32
        ).astype(jnp.bfloat16),
        "seq",
        scatter_dimension=0,
        tiled=True,
    )
    hidden_grad = lax.psum(owned_rows, "vocab").astype(jnp.float32)
    tokens_here = queries.shape[0]
    heads_here = sinks.shape[0]
    owner_rows = final_hidden.shape[0]
    tiles = tokens_here // WINDOW
    scale = HD ** (-0.5)
    kv_index = lax.axis_index("vocab") // 2
    own_keys = lax.dynamic_slice_in_dim(keys, kv_index * HD, HD, 1)
    own_values = lax.dynamic_slice_in_dim(values, kv_index * HD, HD, 1)
    doc_marks = (doc_ids + 1).astype(jnp.bfloat16)
    tail_keys, tail_values, tail_marks = passed_along(
        (own_keys[-WINDOW:], own_values[-WINDOW:], doc_marks[-WINDOW:]), "seq", 1
    )
    ext_keys = jnp.concatenate([tail_keys, own_keys], axis=0)
    ext_values = jnp.concatenate([tail_values, own_values], axis=0)
    ext_marks = jnp.concatenate([tail_marks, doc_marks], axis=0)
    slot_grad = lax.dot_general(
        hidden_grad.astype(jnp.bfloat16),
        out_proj,
        contract_last,
        preferred_element_type=jnp.float32,
    )
    positions = lax.broadcasted_iota(jnp.int32, (tokens_here, owner_rows), 0)
    landing = (positions == slot_pos[None, :]).astype(jnp.float32)
    grad_out = (
        upper_grad.astype(jnp.float32)
        + jnp.dot(landing, slot_grad, preferred_element_type=jnp.float32)
    ).astype(jnp.bfloat16)
    query_tiles = queries.reshape(tiles, WINDOW, heads_here, HD)
    grad_tiles = grad_out.reshape(tiles, WINDOW, heads_here, HD)
    key_strips = strip_rows(ext_keys, tiles, WINDOW)
    value_strips = strip_rows(ext_values, tiles, WINDOW)
    mark_strips = strip_rows(ext_marks, tiles, WINDOW)
    query_marks = doc_marks.reshape(tiles, WINDOW)
    offsets = (
        lax.broadcasted_iota(jnp.int32, (WINDOW, 2 * WINDOW), 0)
        + WINDOW
        - lax.broadcasted_iota(jnp.int32, (WINDOW, 2 * WINDOW), 1)
    )
    band = (offsets >= 0) & (offsets < WINDOW)
    allowed = (band[None] & (query_marks[:, :, None] == mark_strips[:, None, :]))[:, None]
    sink_col = sinks[None, :, None, None]
    scores = (
        jnp.einsum("tqhd,tkd->thqk", query_tiles, key_strips, preferred_element_type=jnp.float32)
        * scale
    )
    masked = jnp.where(allowed, scores, masked_score)
    row_top = jnp.maximum(jnp.max(masked, axis=3, keepdims=True), sink_col)
    exp_terms = jnp.where(allowed, jnp.exp(masked - row_top), 0.0)
    sink_term = jnp.exp(sink_col - row_top)
    total = jnp.sum(exp_terms, axis=3, keepdims=True) + sink_term
    attn_prob = exp_terms / total
    attn_low = attn_prob.astype(jnp.bfloat16)
    attended = jnp.einsum(
        "thqk,tkd->tqhd", attn_low, value_strips, preferred_element_type=jnp.float32
    )
    delta = jnp.transpose(jnp.sum(grad_tiles.astype(jnp.float32) * attended, axis=3), (0, 2, 1))[
        ..., None
    ]
    dprob = jnp.einsum(
        "tqhd,tkd->thqk", grad_tiles, value_strips, preferred_element_type=jnp.float32
    )
    dscore = (attn_prob * (dprob - delta)).astype(jnp.bfloat16)
    grad_queries = (
        (
            jnp.einsum("thqk,tkd->tqhd", dscore, key_strips, preferred_element_type=jnp.float32)
            * scale
        )
        .astype(jnp.bfloat16)
        .reshape(tokens_here, heads_here * HD)
    )
    key_strip_grad = (
        jnp.einsum("thqk,tqhd->tkd", dscore, query_tiles, preferred_element_type=jnp.float32)
        * scale
    )
    value_strip_grad = jnp.einsum(
        "thqk,tqhd->tkd", attn_low, grad_tiles, preferred_element_type=jnp.float32
    )
    edge = jnp.zeros((1, WINDOW, HD), jnp.float32)
    key_grad = (
        jnp.concatenate([key_strip_grad[:, :WINDOW], edge], axis=0)
        + jnp.concatenate([edge, key_strip_grad[:, WINDOW:]], axis=0)
    ).reshape(tokens_here + WINDOW, HD)
    value_grad = (
        jnp.concatenate([value_strip_grad[:, :WINDOW], edge], axis=0)
        + jnp.concatenate([edge, value_strip_grad[:, WINDOW:]], axis=0)
    ).reshape(tokens_here + WINDOW, HD)
    sink_grad = -jnp.sum(sink_term / total * delta, axis=(0, 2, 3))
    back_key, back_value = (
        passed_along(key_grad[:WINDOW].astype(jnp.bfloat16), "seq", -1).astype(jnp.float32),
        passed_along(value_grad[:WINDOW].astype(jnp.bfloat16), "seq", -1).astype(jnp.float32),
    )
    filler = jnp.zeros((tokens_here - WINDOW, HD), jnp.float32)
    own_key = key_grad[WINDOW:] + jnp.concatenate([filler, back_key], axis=0)
    own_value = value_grad[WINDOW:] + jnp.concatenate([filler, back_value], axis=0)
    stacked = jnp.stack([own_key, own_value])
    half_width = HD // 2
    parity = lax.axis_index("vocab") % 2
    outgoing = lax.dynamic_slice_in_dim(stacked, (1 - parity) * half_width, half_width, 2)
    kept_half = lax.dynamic_slice_in_dim(stacked, parity * half_width, half_width, 2)
    received = partner(outgoing.astype(jnp.bfloat16), "vocab", 0).astype(outgoing.dtype)
    grad_kv = jnp.swapaxes(kept_half + received, 1, 2).astype(jnp.bfloat16)
    grad_sinks = lax.psum(sink_grad, "seq")
    return (grad_queries, grad_kv, grad_sinks, hidden_grad)


def solution(mesh):
    in_specs = (
        P("seq", "vocab"),
        P("seq", None),
        P("seq", None),
        P("vocab"),
        P("seq"),
        P("seq", "vocab"),
        P("vocab", None),
        P("seq", None),
        P("seq"),
        P("seq"),
        P("seq"),
        P("seq"),
        P(("seq", "vocab"), None),
        P(("seq", "vocab"), None),
    )
    out_specs = (P("seq", "vocab"), P(None, "vocab", "seq"), P("vocab"), P("seq", None))
    return jax.shard_map(shards, mesh=mesh, in_specs=in_specs, out_specs=out_specs, check_vma=False)
```

profile of v0, /device:TPU:32, one launch (start us, length us, event | category | flops | bytes accessed | tf_op | source)
XLA Modules:
  0.0 630.5 jit_solution(6142529916333679414)
XLA Ops:
  8.0 0.7 add_convert_fusion
  9.3 3.4 collective-permute-start.1
  12.7 1.5 dynamic-slice.6
  14.1 3.4 collective-permute-start.2
  17.5 1.4 dynamic-slice.5
  19.0 3.1 collective-permute-start
  22.1 1.1 constant_dynamic-slice_fusion
  23.4 0.7 copy.60
  24.1 1.2 reshape.118
  27.7 74.0 %all-reduce.7 = bf16[256]{0:T(256)(128)(2,1)S(1)} all-reduce(bf16[256]{0:T(256)(128)(2,1)S(1)} %dynamic-update-slice.1), channel_id=1, replica_groups=mesh['seq'=32,'vocab'=16] {'seq'}, use_global_device_ids=true, to_apply=%add.7 | all-reduce | flops 256 | bytes 1024
  101.7 14.8 %all-reduce.10 = (s32[256]{0:T(256)}, s32[256]{0:T(256)S(1)}) all-reduce(s32[256]{0:T(256)S(1)} %dynamic-update-slice.2, s32[256]{0:T(256)S(1)} %dynamic-update-slice), channel_id=1, replica_groups=mesh['seq'=32,'vocab'=16] {'seq'}, use_global_device_ids=true, to_apply=%add.8 | all-reduce | flops 512 | bytes 4096
  120.2 2.2 fusion.55
  123.1 103.0 %all-reduce.12 = (f32[256]{0:T(256)S(1)}, f32[256]{0:T(256)S(1)}) all-reduce(f32[256]{0:T(256)S(1)} %get-tuple-element.31, f32[256]{0:T(256)S(1)} %get-tuple-element.33), channel_id=1, replica_groups=mesh['seq'=32,'vocab'=16] {'seq','vocab'}, use_global_device_ids=true, to_apply=%region_7.0 | all-reduce | flops 512 | bytes 4096 | tf_op jit(solution)/shard_map/pmax | solution.py:65
  226.1 94.7 %all-reduce.11 = (f32[256]{0:T(256)S(1)}, f32[256]{0:T(256)S(1)}, f32[256]{0:T(256)S(1)}) all-reduce(f32[256]{0:T(256)S(1)} %get-tuple-element.14, f32[256]{0:T(256)S(1)} %get-tuple-element.13, f32[256]{0:T(256)S(1)} %get-tuple-element.12), channel_id=1, replica_groups=mesh['seq'=32,'vocab'=16] {'seq','vocab'}, use_global_device_ids=true, to_apply=%region_9.0 | all-reduce | flops 768 | bytes 6144 | tf_op jit(solution)/shard_map/psum | solution.py:70
  320.9 2.6 convolution_convert_fusion
  323.5 0.7 pad_maximum_fusion.3
  324.2 0.9 compare_and_fusion
  325.1 0.9 pad_maximum_fusion
  326.2 0.8 pad_maximum_fusion.1
  327.7 1.3 copy-done.1
  329.6 150.9 %all-reduce.15.cloned.1.call-done = bf16[256,2880]{1,0:T(8,128)(2,1)} async-done(((bf16[256,2880]{1,0:T(8,128)(2,1)}), bf16[256,2880]{1,0:T(8,128)(2,1)}) %all-reduce.15.cloned.1.call-update) | async-done | bytes 1474576
  480.5 0.8 constant_dynamic-slice_fusion.2
  481.3 46.8 %psum.38 = bf16[8,2880]{1,0:T(8,128)(2,1)S(1)} all-reduce(bf16[8,2880]{1,0:T(8,128)(2,1)S(1)} %constant_dynamic-slice_fusion.2), channel_id=1, replica_groups=mesh['seq'=32,'vocab'=16] {'vocab'}, use_global_device_ids=true, to_apply=%region_13.14 | all-reduce | flops 23040 | bytes 92160 | tf_op jit(solution)/shard_map/psum | solution.py:95
  529.3 2.5 convolution_bitcast_fusion.1
  531.8 0.8 fusion.8
  532.8 0.9 fusion.1
  534.2 4.7 collective-permute-start.3
  538.9 2.7 collective-permute-start.4
  541.6 2.9 collective-permute-done.4
  544.5 1.9 collective-permute-start.5
  546.8 74.2 %psum.39 = f32[4]{0:T(128)} all-reduce(f32[4]{0:T(128)S(1)} %neg.7), channel_id=1, replica_groups=mesh['seq'=32,'vocab'=16] {'seq'}, use_global_device_ids=true, to_apply=%region_16.17 | all-reduce | flops 4 | bytes 32 | tf_op jit(solution)/shard_map/psum | solution.py:197
  622.0 1.0 reshape.116
  (89 shorter events, 12.0 us)
Async XLA Ops:
  7.2 521.0 %copy-start = (bf16[256,2880]{0,1:T(8,128)(2,1)S(1)}, bf16[256,2880]{0,1:T(8,128)(2,1)}, u32[]{:S(2)}) copy-start(bf16[256,2880]{0,1:T(8,128)(2,1)} %param.20) | copy-start | bytes 4423684
  7.2 18.5 %copy-start.13 = (u32[512]{0:T(512)S(1)}, u32[512]{0:T(512)}, u32[]{:S(2)}) copy-start(u32[512]{0:T(512)} %constant.87) | copy-start | bytes 6148
  7.2 111.0 %copy-start.11 = (s32[512]{0:T(512)S(1)}, s32[512]{0:T(512)}, u32[]{:S(2)}) copy-start(s32[512]{0:T(512)} %param.18) | copy-start | bytes 6148
  7.2 19.8 %copy-start.15 = (bf16[8]{0:T(256)(128)(2,1)S(1)}, bf16[8]{0:T(256)(128)(2,1)}, u32[]{:S(2)}) copy-start(bf16[8]{0:T(256)(128)(2,1)} %param.22) | copy-start | bytes 52
  7.2 20.0 %copy-start.16 = (s32[8]{0:T(128)S(1)}, s32[8]{0:T(128)}, u32[]{:S(2)}) copy-start(s32[8]{0:T(128)} %param.25) | copy-start | bytes 100
  7.2 20.3 %copy-start.17 = (s32[8]{0:T(128)S(1)}, s32[8]{0:T(128)}, u32[]{:S(2)}) copy-start(s32[8]{0:T(128)} %param.24) | copy-start | bytes 100
  7.2 112.9 %copy-start.4 = (bf16[200,2880]{1,0:T(8,128)(2,1)S(1)}, bf16[200,2880]{1,0:T(8,128)(2,1)}, u32[]{:S(2)}) copy-start(bf16[200,2880]{1,0:T(8,128)(2,1)} %param.26) | copy-start | bytes 3456004
  7.2 112.9 %all-gather.2.cloned.1.call-start = ((), (), s32[]{:S(2)}) async-start(), calls=%async_computation | async-start | bytes 1554432 | tf_op jit(solution)/shard_map/all_gather | solution.py:49
  8.0 472.5 %all-reduce.15.cloned.1.call-start = ((), (), s32[]{:S(2)}) async-start(), calls=%async_computation.1 | async-start | bytes 3014656
  9.3 110.3 %collective-permute-start.1 = (bf16[128]{0:T(256)(128)(2,1)}, bf16[128]{0:T(256)(128)(2,1)S(1)}, u32[]{:S(2)}, u32[]{:S(2)}) collective-permute-start(bf16[128]{0:T(256)(128)(2,1)} %slice.85), channel_id=1, source_target_pairs={{0,16},{16,32},{32,48},{48,64},{64,80},{80,96},{96,112},{112,128},... | collective-permute-start | bytes 776 | tf_op jit(solution)/shard_map/ppermute | solution.py:20
  14.1 311.0 %collective-permute-start.2 = (bf16[128,64]{1,0:T(8,128)(2,1)}, bf16[128,64]{1,0:T(8,128)(2,1)}, u32[]{:S(2)}, u32[]{:S(2)}) collective-permute-start(bf16[128,64]{1,0:T(8,128)(2,1)} %dynamic-slice.6), channel_id=1, source_target_pairs={{0,16},{16,32},{32,48},{48,64},{64,80},{80,96},{96,112},{112,128},... | collective-permute-start | bytes 49160 | tf_op jit(solution)/shard_map/ppermute | solution.py:20
  19.0 307.2 %collective-permute-start = (bf16[128,64]{1,0:T(8,128)(2,1)}, bf16[128,64]{1,0:T(8,128)(2,1)}, u32[]{:S(2)}, u32[]{:S(2)}) collective-permute-start(bf16[128,64]{1,0:T(8,128)(2,1)} %dynamic-slice.5), channel_id=1, source_target_pairs={{0,16},{16,32},{32,48},{48,64},{64,80},{80,96},{96,112},{112,128},... | collective-permute-start | bytes 49160 | tf_op jit(solution)/shard_map/ppermute | solution.py:20
  23.2 0.9 copy-start.5
  23.3 0.9 copy-start.7
  120.2 2.2 copy-start.3
  120.2 2.2 copy-start.8
  320.9 5.3 copy-start.6
  323.5 4.1 copy-start.12
  327.1 201.1 %copy-start.9 = (bf16[512,256]{1,0:T(8,128)(2,1)S(1)}, bf16[512,256]{1,0:T(8,128)(2,1)}, u32[]{:S(2)}) copy-start(bf16[512,256]{1,0:T(8,128)(2,1)} %param.19) | copy-start | bytes 786436
  327.1 201.1 %copy-start.14 = (s32[8]{0:T(128)S(1)}, s32[8]{0:T(128)}, u32[]{:S(2)}) copy-start(s32[8]{0:T(128)} %param.23) | copy-start | bytes 100
  327.6 1.4 copy-start.1
  529.3 2.5 copy-start.2
  529.3 2.5 copy-start.10
  534.2 7.4 %collective-permute-start.3 = (bf16[128,64]{0,1:T(8,128)(2,1)S(1)}, bf16[128,64]{0,1:T(8,128)(2,1)S(1)}, u32[]{:S(2)}, u32[]{:S(2)}) collective-permute-start(bf16[128,64]{0,1:T(8,128)(2,1)S(1)} %fusion.42), channel_id=1, source_target_pairs={{16,0},{32,16},{48,32},{64,48},{80,64},{96,80},{112,96},{128,112},... | collective-permute-start | bytes 49160 | tf_op jit(solution)/shard_map/ppermute | solution.py:20
  538.9 5.6 collective-permute-start.4
  544.5 78.5 %collective-permute-start.5 = (bf16[2,512,32]{1,2,0:T(8,128)(2,1)S(1)}, bf16[2,512,32]{1,2,0:T(8,128)(2,1)S(1)}, u32[]{:S(2)}, u32[]{:S(2)}) collective-permute-start(bf16[2,512,32]{1,2,0:T(8,128)(2,1)S(1)} %fusion.21), channel_id=1, source_target_pairs={{0,1},{1,0},{2,3},{3,2},{4,5},{5,4},{6,7},{7,6},{8,9},{9,8},{10,11... | collective-permute-start | bytes 196616 | tf_op jit(solution)/shard_map/ppermute | solution.py:24
Sparse Core Ops, SparseCore 0:
  11.2 84.4 all-gather.1
  323.6 156.8 all-reduce.14
where the time goes:
time: 631 us
  blocking collectives  408 us (65%)
  waiting for transfers between devices  155 us (25%)
  starting transfers between devices  19.3 us (3%)
  between operations  15.9 us (3%)
  local copies, waits for them, and re-layouts  13.1 us (2%)
  matrix products  11.4 us (2%)
  other arithmetic  8.71 us (1%)
    unnamed x3, waiting for transfers between devices  152 us
    pmax x1, blocking collectives, shards(): lax.pmax((policy_peak, frozen_peak), ('seq', 'vocab'))  103 us
    psum x1, blocking collectives, shards(): lax.psum((local_mass, local_cross, local_frozen), ('seq', 'vocab'))  94.7 us
    unnamed x2, blocking collectives  88.8 us
    psum x1, blocking collectives, shards(): grad_sinks = lax.psum(sink_grad, 'seq')  74.2 us
    psum x1, blocking collectives, shards(): hidden_grad = lax.psum(owned_rows, 'vocab').astype(jnp.float32)  46.8 us
    ppermute x5, starting transfers between devices, passed_along(): lax.ppermute(value, axis, [(source, source + steps) for source in range(l...  17.3 us
  transfers between devices with their start and end apart: 8, of which 2 were waited for; matrix products, arithmetic and copies ran while one was open for 4% of the time, Pallas kernels for 0%

commit v1 on v0

--- a/solution.py
+++ b/solution.py
@@ -1,17 +1,391 @@
 import jax
 import jax.numpy as jnp
 from jax import lax
+from jax.experimental import pallas as pl
+from jax.experimental.pallas import tpu as pltpu
 from jax.sharding import PartitionSpec as P
 
 HD = 64
 WINDOW = 128
-
+NX, NY, NZ, NC = 4, 8, 8, 2
+D = 2880
+QUARTER = 768
+HALF = 2 * QUARTER
+SLOTS = 8
 
 loss_scale = 64.0
 kl_weight = 1.0
 masked_score = -1e30
 contract_last = (((1,), (1,)), ((), ()))
 contract_first = (((0,), (0,)), ((), ()))
+MESH = pl.DeviceIdType.MESH
+f32 = jnp.float32
+bf16 = jnp.bfloat16
+
+
+def wrap(value, size):
+    return lax.rem(value + size, size)
+
+
+def position():
+    seq, vocab = lax.axis_index("seq"), lax.axis_index("vocab")
+    return lax.rem(seq, NX), lax.div(seq, NX), lax.div(vocab, NC), lax.rem(vocab, NC)
+
+
+def device(x, y, z, c):
+    return (y * NX + x, z * NC + c)
+
+
+def unfold(block, row):
+    return jnp.concatenate([block[row : row + 1], block[row + 3 : row + 4]], axis=1)
+
+
+def fold(rows):
+    half = rows[0].shape[1] // 2
+    parts = [row[:, :half] for row in rows] + [row[:, half:] for row in rows]
+    return jnp.concatenate(parts + [jnp.zeros((2, half), f32)], axis=0)
+
+
+def merged(blocks):
+    rows = [[unfold(block, k) for block in blocks] for k in range(3)]
+    tops = [rows[0][0], rows[1][0]]
+    for k in range(2):
+        for row in rows[k][1:]:
+            tops[k] = jnp.maximum(tops[k], row)
+    mass, cross, frozen = 0.0, 0.0, 0.0
+    for policy, other, mean in zip(*rows):
+        share = jnp.exp(policy - tops[0])
+        mass += share
+        cross += share * mean
+        frozen += jnp.exp(other - tops[1])
+    return [tops[0] + jnp.log(mass), tops[1] + jnp.log(frozen), cross / mass]
+
+
+def head_kernel(
+    hidden_ref,
+    meta_ref,
+    policy_hbm,
+    frozen_hbm,
+    out_ref,
+    policy_ref,
+    frozen_ref,
+    wide,
+    gathered,
+    rows_ref,
+    meta_y,
+    meta_x,
+    stat_xc,
+    stat_y,
+    stat_z,
+    total,
+    outgoing,
+    from_core,
+    send_x,
+    from_x,
+    send_y,
+    from_y,
+    from_z,
+    final,
+    load_sem,
+    gy_s,
+    gy_r,
+    gx_s,
+    gx_r,
+    gc_s,
+    gc_r,
+    my_s,
+    my_r,
+    mx_s,
+    mx_r,
+    sx_s,
+    sx_r,
+    sy_s,
+    sy_r,
+    sz_s,
+    sz_r,
+    rc_s,
+    rc_r,
+    rx_s,
+    rx_r,
+    ry_s,
+    ry_r,
+    rz_s,
+    rz_r,
+    fc_s,
+    fc_r,
+):
+    x, y, z, c = position()
+    vocab_rows = policy_ref.shape[0]
+    load_policy = pltpu.make_async_copy(policy_hbm, policy_ref, load_sem.at[0])
+    load_frozen = pltpu.make_async_copy(frozen_hbm, frozen_ref, load_sem.at[1])
+    load_policy.start()
+    load_frozen.start()
+
+    def along_x(d, other):
+        return device(wrap(x + d, NX), y, z, c if other == 0 else 1 - c)
+
+    def along_y(d):
+        return device(x, wrap(y + d, NY), z, c)
+
+    def along_z(d):
+        return device(x, y, wrap(z + d, NZ), c)
+
+    across = device(x, y, z, 1 - c)
+    xc_steps = [(d, o) for d in range(NX) for o in range(NC) if d or o]
+
+    def send(src, dst, send_sem, recv_sem, target):
+        copy = pltpu.make_async_remote_copy(
+            src_ref=src,
+            dst_ref=dst,
+            send_sem=send_sem,
+            recv_sem=recv_sem,
+            device_id=target,
+            device_id_type=MESH,
+        )
+        copy.start()
+        return copy
+
+    barrier = pltpu.get_barrier_semaphore()
+    peers = [along_x(d, o) for d, o in xc_steps]
+    peers += [along_y(d) for d in range(1, NY)] + [along_z(d) for d in range(1, NZ)]
+    for peer in peers:
+        pl.semaphore_signal(barrier, inc=1, device_id=peer, device_id_type=MESH)
+
+    hidden = hidden_ref[...].astype(f32)
+    wide[3] = jnp.zeros((SLOTS, QUARTER), f32)
+    for q in range(4):
+        stop = min(D, (q + 1) * QUARTER)
+        wide[q, :, : stop - q * QUARTER] = hidden[:, q * QUARTER : stop]
+    gathered[c, x, y] = jnp.concatenate([wide[2 * c], wide[2 * c + 1]], axis=0).astype(bf16)
+    meta_y[y] = meta_ref[...]
+    pl.semaphore_wait(barrier, len(peers))
+
+    copies_y = [
+        send(gathered.at[c, x, y], gathered.at[c, x, y], gy_s.at[d], gy_r.at[d], along_y(d))
+        for d in range(1, NY)
+    ]
+    metas_y = [
+        send(meta_y.at[y], meta_y.at[y], my_s.at[d], my_r.at[d], along_y(d)) for d in range(1, NY)
+    ]
+    for copy in copies_y:
+        copy.wait()
+    copies_x = [
+        send(gathered.at[c, x], gathered.at[c, x], gx_s.at[d], gx_r.at[d], along_x(d, 0))
+        for d in range(1, NX)
+    ]
+
+    def cross_send(group):
+        return send(
+            gathered.at[c, group], gathered.at[c, group], gc_s.at[group], gc_r.at[group], across
+        )
+
+    def arrange(half, group):
+        block = gathered[half, group].astype(f32).reshape(NY, 2, SLOTS, QUARTER)
+        start = pl.multiple_of(group * (NY * SLOTS), NY * SLOTS)
+        for part in range(2):
+            rows_ref[2 * half + part, pl.ds(start, NY * SLOTS), :] = (
+                block[:, part].reshape(NY * SLOTS, QUARTER).astype(bf16)
+            )
+
+    copies_c = [cross_send(x)]
+    arrange(c, x)
+    for copy in metas_y:
+        copy.wait()
+    meta = meta_y[0]
+    for k in range(1, NY):
+        meta += meta_y[k]
+    meta_x[x] = meta
+    metas_x = [
+        send(meta_x.at[x], meta_x.at[x], mx_s.at[d], mx_r.at[d], along_x(d, 0))
+        for d in range(1, NX)
+    ]
+    for d in range(1, NX):
+        copies_x[d - 1].wait()
+        group = wrap(x - d, NX)
+        copies_c.append(cross_send(group))
+        arrange(c, group)
+    for d, copy in enumerate(copies_c):
+        group = wrap(x - d, NX)
+        pltpu.make_async_remote_copy(
+            src_ref=gathered.at[1 - c, group],
+            dst_ref=gathered.at[1 - c, group],
+            send_sem=gc_s.at[group],
+            recv_sem=gc_r.at[group],
+            device_id=across,
+            device_id_type=MESH,
+        ).wait_recv()
+        arrange(1 - c, group)
+    for copy in copies_c:
+        copy.wait_send()
+    for copy in metas_x:
+        copy.wait()
+    meta = meta_x[0]
+    for k in range(1, NX):
+        meta += meta_x[k]
+
+    load_policy.wait()
+    load_frozen.wait()
+
+    def logits_of(head):
+        result = 0.0
+        for q in range(4):
+            stop = min(D, (q + 1) * QUARTER)
+            result += lax.dot_general(
+                head[:, q * QUARTER : stop],
+                rows_ref[q, :, : stop - q * QUARTER],
+                contract_last,
+                preferred_element_type=f32,
+            )
+        return result
+
+    policy_logits = logits_of(policy_ref)
+    frozen_logits = logits_of(frozen_ref)
+    policy_peak = jnp.max(policy_logits, axis=0, keepdims=True)
+    frozen_peak = jnp.max(frozen_logits, axis=0, keepdims=True)
+    logit_diff = policy_logits - frozen_logits
+    policy_terms = jnp.exp(policy_logits - policy_peak)
+    mass = jnp.sum(policy_terms, axis=0, keepdims=True)
+    mean = jnp.sum(policy_terms * logit_diff, axis=0, keepdims=True) / mass
+    frozen_mass = jnp.sum(jnp.exp(frozen_logits - frozen_peak), axis=0, keepdims=True)
+    stats = [policy_peak + jnp.log(mass), frozen_peak + jnp.log(frozen_mass), mean]
+
+    stat_xc[0] = fold(stats)
+    copies = [
+        send(stat_xc.at[0], stat_xc.at[k + 1], sx_s.at[k], sx_r.at[k], along_x(d, o))
+        for k, (d, o) in enumerate(xc_steps)
+    ]
+    for copy in copies:
+        copy.wait()
+    stat_y[0] = fold(merged([stat_xc[k] for k in range(NX * NC)]))
+    copies = [
+        send(stat_y.at[0], stat_y.at[d], sy_s.at[d], sy_r.at[d], along_y(d)) for d in range(1, NY)
+    ]
+    for copy in copies:
+        copy.wait()
+    stat_z[0] = fold(merged([stat_y[k] for k in range(NY)]))
+    copies = [
+        send(stat_z.at[0], stat_z.at[d], sz_s.at[d], sz_r.at[d], along_z(d)) for d in range(1, NZ)
+    ]
+    for copy in copies:
+        copy.wait()
+    policy_lognorm, frozen_lognorm, cross_total = merged([stat_z[k] for k in range(NZ)])
+
+    divergence = cross_total - policy_lognorm + frozen_lognorm
+    policy_prob = jnp.exp(policy_logits - policy_lognorm)
+    first_id = (lax.axis_index("seq") * (NZ * NC) + lax.axis_index("vocab")) * vocab_rows
+    ids_here = (first_id + lax.broadcasted_iota(jnp.int32, policy_logits.shape, 0)).astype(f32)
+    picked = (ids_here == unfold(meta, 1)).astype(f32)
+    weight = loss_scale * unfold(meta, 2)
+    log_ratio = policy_logits - policy_lognorm - (frozen_logits - frozen_lognorm) - divergence
+    logit_grad = (
+        weight * (-unfold(meta, 0) * (picked - policy_prob) + kl_weight * policy_prob * log_ratio)
+    ).astype(bf16)
+
+    total[1, :, QUARTER:] = jnp.zeros((total.shape[1], QUARTER), f32)
+    for q in range(4):
+        stop = min(D, (q + 1) * QUARTER)
+        half, low = q // 2, (q % 2) * QUARTER
+        total[half, :, low : low + stop - q * QUARTER] = lax.dot_general(
+            logit_grad, policy_ref[:, q * QUARTER : stop], contract_first, preferred_element_type=f32
+        )
+    outgoing[...] = total[1 - c].astype(bf16)
+    copy = send(outgoing, from_core, rc_s, rc_r, across)
+    copy.wait()
+    group_rows = NY * SLOTS
+    for g in range(NX):
+        rows = slice(g * group_rows, (g + 1) * group_rows)
+        both = total[c, rows, :] + from_core[rows, :].astype(f32)
+        total[c, rows, :] = both
+        send_x[g] = both.astype(bf16)
+    copies = [
+        send(send_x.at[wrap(x + d, NX)], from_x.at[d - 1], rx_s.at[d], rx_r.at[d], along_x(d, 0))
+        for d in range(1, NX)
+    ]
+    for copy in copies:
+        copy.wait()
+    mine = total[c, pl.ds(pl.multiple_of(x * group_rows, group_rows), group_rows), :]
+    for k in range(NX - 1):
+        mine += from_x[k].astype(f32)
+    mine = mine.reshape(NY, SLOTS, HALF)
+    packed = jnp.concatenate([mine[:, :, :QUARTER], mine[:, :, QUARTER:]], axis=1)
+    send_y[...] = packed.astype(bf16)
+    copies = [
+        send(send_y.at[wrap(y + d, NY)], from_y.at[d - 1], ry_s.at[d], ry_r.at[d], along_y(d))
+        for d in range(1, NY)
+    ]
+    for copy in copies:
+        copy.wait()
+    summed = send_y[y].astype(f32)
+    for k in range(NY - 1):
+        summed += from_y[k].astype(f32)
+    from_z[z] = summed.astype(bf16)
+    copies = [
+        send(from_z.at[z], from_z.at[z], rz_s.at[d], rz_r.at[d], along_z(d)) for d in range(1, NZ)
+    ]
+    for copy in copies:
+        copy.wait()
+    summed = from_z[0].astype(f32)
+    for k in range(1, NZ):
+        summed += from_z[k].astype(f32)
+    final[c] = summed
+    copy = send(final.at[c], final.at[c], fc_s, fc_r, across)
+    copy.wait()
+    for q in range(4):
+        stop = min(D, (q + 1) * QUARTER)
+        part = final[q // 2, (q % 2) * SLOTS : (q % 2 + 1) * SLOTS, :]
+        out_ref[:, q * QUARTER : stop] = part[:, : stop - q * QUARTER]
+
+
+def head_gradient(final_hidden, advantages, slot_live, sampled_ids, policy_head, reference_head):
+    x, y, _, _ = position()
+    rows = NX * NY * SLOTS
+    values = jnp.stack([advantages.astype(f32), sampled_ids.astype(f32), slot_live.astype(f32)])
+    here = lax.broadcasted_iota(jnp.int32, (3, rows), 1) // SLOTS == x * NY + y
+    placed = jnp.where(here, jnp.tile(values, (1, NX * NY)), 0.0)
+    meta = jnp.concatenate(
+        [placed[:, : rows // 2], placed[:, rows // 2 :], jnp.zeros((2, rows // 2), f32)], axis=0
+    )
+    dma = pltpu.SemaphoreType.DMA
+    vmem = pl.BlockSpec(memory_space=pltpu.VMEM)
+    stat = (8, rows // 2)
+    scratch = [
+        pltpu.VMEM(policy_head.shape, bf16),
+        pltpu.VMEM(reference_head.shape, bf16),
+        pltpu.VMEM((4, SLOTS, QUARTER), f32),
+        pltpu.VMEM((2, NX, NY, 2 * SLOTS, QUARTER), bf16),
+        pltpu.VMEM((4, rows, QUARTER), bf16),
+        pltpu.VMEM((NY,) + stat, f32),
+        pltpu.VMEM((NX,) + stat, f32),
+        pltpu.VMEM((NX * NC,) + stat, f32),
+        pltpu.VMEM((NY,) + stat, f32),
+        pltpu.VMEM((NZ,) + stat, f32),
+        pltpu.VMEM((2, rows, HALF), f32),
+        pltpu.VMEM((rows, HALF), bf16),
+        pltpu.VMEM((rows, HALF), bf16),
+        pltpu.VMEM((NX, NY * SLOTS, HALF), bf16),
+        pltpu.VMEM((NX - 1, NY * SLOTS, HALF), bf16),
+        pltpu.VMEM((NY, 2 * SLOTS, QUARTER), bf16),
+        pltpu.VMEM((NY - 1, 2 * SLOTS, QUARTER), bf16),
+        pltpu.VMEM((NZ, 2 * SLOTS, QUARTER), bf16),
+        pltpu.VMEM((2, 2 * SLOTS, QUARTER), f32),
+        dma((2,)),
+    ]
+    for size in (NY, NX, NX, NY, NX, NX * NC, NY, NZ):
+        scratch += [dma((size,)), dma((size,))]
+    scratch += [dma, dma]
+    for size in (NX, NY, NZ):
+        scratch += [dma((size,)), dma((size,))]
+    scratch += [dma, dma]
+    return pl.pallas_call(
+        head_kernel,
+        out_shape=jax.ShapeDtypeStruct(final_hidden.shape, f32),
+        in_specs=[vmem, vmem, pl.BlockSpec(memory_space=pl.ANY), pl.BlockSpec(memory_space=pl.ANY)],
+        out_specs=vmem,
+        scratch_shapes=scratch,
+        compiler_params=pltpu.CompilerParams(
+            collective_id=0, has_side_effects=True, vmem_limit_bytes=48 * 2**20
+        ),
+    )(final_hidden, meta, policy_head, reference_head)
 
 
 def passed_along(value, axis, steps):
@@ -45,54 +419,9 @@
     policy_head,
     reference_head,
 ):
-    rows_hidden, rows_advantage = (
-        lax.all_gather(final_hidden, "seq", axis=0, tiled=True),
-        lax.all_gather(advantages, "seq", axis=0, tiled=True),
-    )
-    rows_ids, rows_live = (
-        lax.all_gather(sampled_ids, "seq", axis=0, tiled=True),
-        lax.all_gather(slot_live, "seq", axis=0, tiled=True),
-    )
-    policy_logits = lax.dot_general(
-        policy_head, rows_hidden, contract_last, preferred_element_type=jnp.float32
-    )
-    frozen_logits = lax.dot_general(
-        reference_head, rows_hidden, contract_last, preferred_element_type=jnp.float32
-    )
-    policy_peak = jnp.max(policy_logits, axis=0)
-    frozen_peak = jnp.max(frozen_logits, axis=0)
-    logit_diff = policy_logits - frozen_logits
-    top_policy, top_frozen = lax.pmax((policy_peak, frozen_peak), ("seq", "vocab"))
-    policy_terms = jnp.exp(policy_logits - top_policy)
-    local_mass = jnp.sum(policy_terms, axis=0)
-    local_cross = jnp.sum(policy_terms * logit_diff, axis=0)
-    local_frozen = jnp.sum(jnp.exp(frozen_logits - top_frozen), axis=0)
-    total_mass, total_cross, total_frozen = lax.psum(
-        (local_mass, local_cross, local_frozen), ("seq", "vocab")
-    )
-    policy_lognorm = top_policy + jnp.log(total_mass)
-    frozen_lognorm = top_frozen + jnp.log(total_frozen)
-    policy_prob = jnp.exp(policy_logits - policy_lognorm)
-    cross_total = total_cross / total_mass
-    divergence = cross_total - policy_lognorm + frozen_lognorm
-    first_id = lax.axis_index(("seq", "vocab")) * policy_head.shape[0]
-    ids_here = first_id + lax.broadcasted_iota(jnp.int32, policy_logits.shape, 0)
-    picked = (ids_here == rows_ids[None, :]).astype(jnp.float32)
-    weight = loss_scale * rows_live.astype(jnp.float32)
-    advantage_rows = rows_advantage.astype(jnp.float32)
-    log_ratio = policy_logits - policy_lognorm - (frozen_logits - frozen_lognorm) - divergence
-    logit_grad = (
-        weight * (-advantage_rows * (picked - policy_prob) + kl_weight * policy_prob * log_ratio)
-    ).astype(jnp.bfloat16)
-    owned_rows = lax.psum_scatter(
-        lax.dot_general(
-            logit_grad, policy_head, contract_first, preferred_element_type=jnp.float32
-        ).astype(jnp.bfloat16),
-        "seq",
-        scatter_dimension=0,
-        tiled=True,
-    )
-    hidden_grad = lax.psum(owned_rows, "vocab").astype(jnp.float32)
+    hidden_grad = head_gradient(
+        final_hidden, advantages, slot_live, sampled_ids, policy_head, reference_head
+    )
     tokens_here = queries.shape[0]
     heads_here = sinks.shape[0]
     owner_rows = final_hidden.shape[0]

time: 631 us -> 200 us (0.32)
  blocking collectives: 408 us -> 74.3 us
  waiting for transfers between devices: 155 us -> 2.83 us
  Pallas kernels: 0 us -> 74.7 us
  between operations: 15.9 us -> 1.08 us
    unnamed x3 -> x0, waiting for transfers between devices: 152 us -> none
    psum x2 -> x0, blocking collectives: 142 us -> none  [the longest x1 94.7 us: shards(): lax.psum((local_mass, local_cross, local_frozen), ('seq', 'vocab'))]
    pmax x1 -> x0, blocking collectives: 103 us -> none  [shards(): lax.pmax((policy_peak, frozen_peak), ('seq', 'vocab'))]
    unnamed x2 -> x0, blocking collectives: 88.8 us -> none
    pallas_call x0 -> x1, Pallas kernels: none -> 74.7 us  [head_gradient(): pl.pallas_call(head_kernel, out_shape=jax.ShapeDtypeStruct(final_hidden.s...]
  transfers between devices with their start and end apart: 8 -> 6, of which waited for: 2 -> 1; matrix products, arithmetic and copies ran while one was open for 4% -> 10% of each run, Pallas kernels for 0% -> 38%
where the time goes in v1:
time: 200 us; the launch traced here: 199 us
  Pallas kernels  74.7 us (37%)
  blocking collectives  74.3 us (37%)
  starting transfers between devices  17 us (8%)
  local copies, waits for them, and re-layouts  12.6 us (6%)
  other arithmetic  9.84 us (5%)
  matrix products  6.66 us (3%)
  waiting for transfers between devices  2.83 us (1%)
    pallas_call x1, Pallas kernels, head_gradient(): pl.pallas_call(head_kernel, out_shape=jax.ShapeDtypeStruct(final_hidden.s...  74.7 us
    psum x1, blocking collectives, shards(): grad_sinks = lax.psum(sink_grad, 'seq')  74.3 us
    ppermute x5, starting transfers between devices, passed_along(): lax.ppermute(value, axis, [(source, source + steps) for source in range(l...  15 us
    unnamed x33, local copies, waits for them, and re-layouts  4.56 us
  transfers between devices with their start and end apart: 6, of which 1 were waited for; matrix products, arithmetic and copies ran while one was open for 10% of the time, Pallas kernels for 38%

profile of v1, /device:TPU:32, one launch (start us, length us, event | category | flops | bytes accessed | tf_op | source)
XLA Modules:
  0.0 198.9 jit_solution(4845866119667482779)
XLA Ops:
  0.7 1.6 dynamic-slice
  2.3 3.4 %collective-permute-start = (bf16[128,64]{1,0:T(8,128)(2,1)}, bf16[128,64]{1,0:T(8,128)(2,1)}, u32[]{:S(2)}, u32[]{:S(2)}) collective-permute-start(bf16[128,64]{1,0:T(8,128)(2,1)} %dynamic-slice), channel_id=1, source_target_pairs={{0,16},{16,32},{32,48},{48,64},{64,80},{80,96},{96,112},{112,128},... | collective-permute-start | bytes 49160 | tf_op jit(solution)/shard_map/ppermute | solution.py:394
  5.7 0.7 add_convert_fusion
  6.9 3.4 %collective-permute-start.1 = (bf16[128]{0:T(256)(128)(2,1)}, bf16[128]{0:T(256)(128)(2,1)}, u32[]{:S(2)}, u32[]{:S(2)}) collective-permute-start(bf16[128]{0:T(256)(128)(2,1)} %slice.91), channel_id=1, source_target_pairs={{0,16},{16,32},{32,48},{48,64},{64,80},{80,96},{96,112},{112,128},... | collective-permute-start | bytes 776 | tf_op jit(solution)/shard_map/ppermute | solution.py:394
  10.3 1.5 dynamic-slice.1
  11.8 3.1 %collective-permute-start.2 = (bf16[128,64]{1,0:T(8,128)(2,1)}, bf16[128,64]{1,0:T(8,128)(2,1)}, u32[]{:S(2)}, u32[]{:S(2)}) collective-permute-start(bf16[128,64]{1,0:T(8,128)(2,1)} %dynamic-slice.1), channel_id=1, source_target_pairs={{0,16},{16,32},{32,48},{48,64},{64,80},{80,96},{96,112},{112,128},... | collective-permute-start | bytes 49160 | tf_op jit(solution)/shard_map/ppermute | solution.py:394
  14.9 1.8 constant_dynamic-slice_fusion
  16.7 1.3 fusion.56
  17.9 0.6 iota_shift-right-logical_fusion
  19.1 0.7 fusion.29
  19.8 1.2 reshape.99
  21.3 0.7 bitcast_convert_fusion
  22.0 0.7 convert_bitcast_fusion
  22.8 0.7 fusion.39
  23.6 1.3 copy-done.2
  24.9 74.7 %shard_map.165 = f32[8,2880]{1,0:T(8,128)S(1)} custom-call(bf16[8,2880]{1,0:T(8,128)(2,1)S(1)} %copy-done.3, f32[8,128]{1,0:T(8,128)S(1)} %maximum_maximum_fusion.meta_ref, bf16[200,2880]{1,0:T(8,128)(2,1)S(1)} %copy-done.1, bf16[200,2880]{1,0:T(8,128)(2,1)S(1)} %copy-done.2), custom_call_target="tpu_custom_call" | custom-call | tf_op jit(solution)/shard_map/pallas_call | solution.py:379
  99.6 1.3 fusion.6
  101.6 0.6 pad_maximum_fusion.2
  102.5 0.8 pad_maximum_fusion.1
  104.0 1.2 copy-done.4
  105.9 0.8 pad_maximum_fusion
  106.8 2.5 %convolution_bitcast_fusion.1 = f32[4,256,64]{1,2,0:T(8,128)S(1)} fusion(bf16[4,128,4,64]{1,3,2,0:T(8,128)(2,1)S(1)} %copy.39, f32[4,256,128,4]{2,1,3,0:T(8,128)} %copy-done.4, f32[4,4,128]{2,1,0:T(4,128)S(1)} %fusion.38, f32[4,4,128]{2,1,0:T(4,128)S(1)} %broadcast_maximum_fusion, pred[4,128,256]{1,2,0:T(8,128)(4,1)S(1)} %compare_and_fusion), kind=kOutput, calls=%fused_computation.15 | convolution fusion | flops 70254592 | bytes 2768896 | tf_op jit(solution)/shard_map/thqk,tqhd->tkd/dot_general | solution.py:499
  109.3 0.8 fusion.8
  110.3 2.4 %collective-permute-start.4 = (bf16[128,64]{0,1:T(8,128)(2,1)S(1)}, bf16[128,64]{0,1:T(8,128)(2,1)S(1)}, u32[]{:S(2)}, u32[]{:S(2)}) collective-permute-start(bf16[128,64]{0,1:T(8,128)(2,1)S(1)} %fusion.37), channel_id=1, source_target_pairs={{16,0},{32,16},{48,32},{64,48},{80,64},{96,80},{112,96},{128,112},... | collective-permute-start | bytes 49160 | tf_op jit(solution)/shard_map/ppermute | solution.py:394
  112.7 0.9 fusion.1
  114.1 2.8 %collective-permute-start.3 = (bf16[128,64]{0,1:T(8,128)(2,1)S(1)}, bf16[128,64]{0,1:T(8,128)(2,1)S(1)}, u32[]{:S(2)}, u32[]{:S(2)}) collective-permute-start(bf16[128,64]{0,1:T(8,128)(2,1)S(1)} %fusion.36), channel_id=1, source_target_pairs={{16,0},{32,16},{48,32},{64,48},{80,64},{96,80},{112,96},{128,112},... | collective-permute-start | bytes 49160 | tf_op jit(solution)/shard_map/ppermute | solution.py:394
  116.9 2.8 %collective-permute-done.3 = bf16[128,64]{0,1:T(8,128)(2,1)S(1)} collective-permute-done((bf16[128,64]{0,1:T(8,128)(2,1)S(1)}, bf16[128,64]{0,1:T(8,128)(2,1)S(1)}, u32[]{:S(2)}, u32[]{:S(2)}) %collective-permute-start.3) | collective-permute-done | bytes 16416 | tf_op jit(solution)/shard_map/ppermute | solution.py:394
  119.7 1.9 collective-permute-start.5
  122.0 74.3 %psum.7 = f32[4]{0:T(128)} all-reduce(f32[4]{0:T(128)S(1)} %neg.3), channel_id=1, replica_groups=mesh['seq'=32,'vocab'=16] {'seq'}, use_global_device_ids=true, to_apply=%region_4.5 | all-reduce | flops 4 | bytes 32 | tf_op jit(solution)/shard_map/psum | solution.py:526
  196.6 1.0 reshape.98
  197.6 0.6 fusion.31
  198.3 0.6 copy.78
  (69 shorter events, 5.4 us)
Async XLA Ops:
  0.6 98.9 %copy-start = (bf16[256,2880]{0,1:T(8,128)(2,1)S(1)}, bf16[256,2880]{0,1:T(8,128)(2,1)}, u32[]{:S(2)}) copy-start(bf16[256,2880]{0,1:T(8,128)(2,1)} %param.20) | copy-start | bytes 4423684
  0.6 23.0 %copy-start.3 = (bf16[8,2880]{1,0:T(8,128)(2,1)S(1)}, bf16[8,2880]{1,0:T(8,128)(2,1)}, u32[]{:S(2)}) copy-start(bf16[8,2880]{1,0:T(8,128)(2,1)} %hidden_ref.1) | copy-start | bytes 138244
  0.7 23.0 %copy-start.1 = (bf16[200,2880]{1,0:T(8,128)(2,1)S(1)}, bf16[200,2880]{1,0:T(8,128)(2,1)}, u32[]{:S(2)}) copy-start(bf16[200,2880]{1,0:T(8,128)(2,1)} %policy_hbm.1) | copy-start | bytes 3456004
  2.3 100.2 %collective-permute-start = (bf16[128,64]{1,0:T(8,128)(2,1)}, bf16[128,64]{1,0:T(8,128)(2,1)}, u32[]{:S(2)}, u32[]{:S(2)}) collective-permute-start(bf16[128,64]{1,0:T(8,128)(2,1)} %dynamic-slice), channel_id=1, source_target_pairs={{0,16},{16,32},{32,48},{48,64},{64,80},{80,96},{96,112},{112,128},... | collective-permute-start | bytes 49160 | tf_op jit(solution)/shard_map/ppermute | solution.py:394
  6.4 5.4 %copy-start.13 = (bf16[512]{0:T(512)(128)(2,1)}, bf16[512]{0:T(512)(128)(2,1)S(1)}, u32[]{:S(2)}) copy-start(bf16[512]{0:T(512)(128)(2,1)S(1)} %add_convert_fusion) | copy-start | bytes 3076
  6.9 94.7 %collective-permute-start.1 = (bf16[128]{0:T(256)(128)(2,1)}, bf16[128]{0:T(256)(128)(2,1)}, u32[]{:S(2)}, u32[]{:S(2)}) collective-permute-start(bf16[128]{0:T(256)(128)(2,1)} %slice.91), channel_id=1, source_target_pairs={{0,16},{16,32},{32,48},{48,64},{64,80},{80,96},{96,112},{112,128},... | collective-permute-start | bytes 776 | tf_op jit(solution)/shard_map/ppermute | solution.py:394
  11.8 94.1 %collective-permute-start.2 = (bf16[128,64]{1,0:T(8,128)(2,1)}, bf16[128,64]{1,0:T(8,128)(2,1)}, u32[]{:S(2)}, u32[]{:S(2)}) collective-permute-start(bf16[128,64]{1,0:T(8,128)(2,1)} %dynamic-slice.1), channel_id=1, source_target_pairs={{0,16},{16,32},{32,48},{48,64},{64,80},{80,96},{96,112},{112,128},... | collective-permute-start | bytes 49160 | tf_op jit(solution)/shard_map/ppermute | solution.py:394
  16.7 3.2 %copy-start.7 = (bf16[512,64]{1,0:T(8,128)(2,1)}, bf16[512,64]{1,0:T(8,128)(2,1)S(1)}, u32[]{:S(2)}) copy-start(bf16[512,64]{1,0:T(8,128)(2,1)S(1)} %get-tuple-element.21) | copy-start | bytes 196612
  23.6 1.3 copy-start.2
  24.9 74.7 %copy-start.9 = (bf16[512,256]{1,0:T(8,128)(2,1)S(1)}, bf16[512,256]{1,0:T(8,128)(2,1)}, u32[]{:S(2)}) copy-start(bf16[512,256]{1,0:T(8,128)(2,1)} %param.19) | copy-start | bytes 786436
  24.9 76.0 %copy-start.6 = (bf16[512,64]{1,0:T(8,128)(2,1)S(1)}, bf16[512,64]{1,0:T(8,128)(2,1)}, u32[]{:S(2)}) copy-start(bf16[512,64]{1,0:T(8,128)(2,1)} %get-tuple-element.20) | copy-start | bytes 196612
  99.6 2.0 %copy-start.14 = (bf16[512]{0:T(512)(128)(2,1)S(1)}, bf16[512]{0:T(512)(128)(2,1)}, u32[]{:S(2)}) copy-start(bf16[512]{0:T(512)(128)(2,1)} %copy-done.13) | copy-start | bytes 3076
  99.6 2.7 %copy-start.11 = (bf16[4,128]{1,0:T(4,128)(2,1)S(1)}, bf16[4,128]{1,0:T(4,128)(2,1)}, u32[]{:S(2)}) copy-start(bf16[4,128]{1,0:T(4,128)(2,1)} %fusion.56) | copy-start | bytes 3076
  99.6 2.7 %copy-start.10 = (pred[128,256]{0,1:T(8,128)(4,1)S(1)}, pred[128,256]{0,1:T(8,128)(4,1)}, u32[]{:S(2)}) copy-start(pred[128,256]{0,1:T(8,128)(4,1)} %fusion.29) | copy-start | bytes 98308
  99.6 2.9 %copy-start.8 = (bf16[512,64]{1,0:T(8,128)(2,1)S(1)}, bf16[512,64]{1,0:T(8,128)(2,1)}, u32[]{:S(2)}) copy-start(bf16[512,64]{1,0:T(8,128)(2,1)} %copy-done.7) | copy-start | bytes 196612
  101.3 2.6 %copy-start.12 = (f32[4]{0:T(128)S(1)}, f32[4]{0:T(128)}, u32[]{:S(2)}) copy-start(f32[4]{0:T(128)} %param.17) | copy-start | bytes 52
  103.9 1.3 copy-start.4
  106.8 2.5 %copy-start.5 = (f32[4,256,128,4]{2,1,3,0:T(8,128)S(1)}, f32[4,256,128,4]{2,1,3,0:T(8,128)}, u32[]{:S(2)}) copy-start(f32[4,256,128,4]{2,1,3,0:T(8,128)} %copy-done.4) | copy-start | bytes 6291460
  110.3 6.6 %collective-permute-start.4 = (bf16[128,64]{0,1:T(8,128)(2,1)S(1)}, bf16[128,64]{0,1:T(8,128)(2,1)S(1)}, u32[]{:S(2)}, u32[]{:S(2)}) collective-permute-start(bf16[128,64]{0,1:T(8,128)(2,1)S(1)} %fusion.37), channel_id=1, source_target_pairs={{16,0},{32,16},{48,32},{64,48},{80,64},{96,80},{112,96},{128,112},... | collective-permute-start | bytes 49160 | tf_op jit(solution)/shard_map/ppermute | solution.py:394
  114.1 5.6 %collective-permute-start.3 = (bf16[128,64]{0,1:T(8,128)(2,1)S(1)}, bf16[128,64]{0,1:T(8,128)(2,1)S(1)}, u32[]{:S(2)}, u32[]{:S(2)}) collective-permute-start(bf16[128,64]{0,1:T(8,128)(2,1)S(1)} %fusion.36), channel_id=1, source_target_pairs={{16,0},{32,16},{48,32},{64,48},{80,64},{96,80},{112,96},{128,112},... | collective-permute-start | bytes 49160 | tf_op jit(solution)/shard_map/ppermute | solution.py:394
  119.7 77.9 %collective-permute-start.5 = (bf16[2,512,32]{1,2,0:T(8,128)(2,1)S(1)}, bf16[2,512,32]{1,2,0:T(8,128)(2,1)S(1)}, u32[]{:S(2)}, u32[]{:S(2)}) collective-permute-start(bf16[2,512,32]{1,2,0:T(8,128)(2,1)S(1)} %fusion.20), channel_id=1, source_target_pairs={{0,1},{1,0},{2,3},{3,2},{4,5},{5,4},{6,7},{7,6},{8,9},{9,8},{10,11... | collective-permute-start | bytes 196616 | tf_op jit(solution)/shard_map/ppermute | solution.py:398

commit v2 on v0

v2 whole, which is shorter than its diff:
```python
import jax
import jax.numpy as jnp
from jax import lax
from jax.experimental import pallas as pl
from jax.experimental.pallas import tpu as pltpu
from jax.sharding import PartitionSpec as P

HD = 64
WINDOW = 128
NX, NY, NZ, NC = 4, 8, 8, 2
D = 2880
QUARTER = 768
HALF = 2 * QUARTER
SLOTS = 8
PART = NY // 2

loss_scale = 64.0
kl_weight = 1.0
masked_score = -1e30
contract_last = (((1,), (1,)), ((), ()))
contract_first = (((0,), (0,)), ((), ()))
MESH = pl.DeviceIdType.MESH
f32 = jnp.float32
bf16 = jnp.bfloat16


def wrap(value, size):
    return lax.rem(value + size, size)


def device(x, y, z, c):
    return (y * NX + x, z * NC + c)


def unfold(block, row):
    return jnp.concatenate([block[row : row + 1], block[row + 3 : row + 4]], axis=1)


def fold(rows):
    half = rows[0].shape[1] // 2
    parts = [row[:, :half] for row in rows] + [row[:, half:] for row in rows]
    return jnp.concatenate(parts + [jnp.zeros((2, half), f32)], axis=0)


def merged(blocks):
    rows = [[unfold(block, k) for block in blocks] for k in range(3)]
    tops = [rows[0][0], rows[1][0]]
    for k in range(2):
        for row in rows[k][1:]:
            tops[k] = jnp.maximum(tops[k], row)
    mass, cross, frozen = 0.0, 0.0, 0.0
    for policy, other, mean in zip(*rows):
        share = jnp.exp(policy - tops[0])
        mass += share
        cross += share * mean
        frozen += jnp.exp(other - tops[1])
    return [tops[0] + jnp.log(mass), tops[1] + jnp.log(frozen), cross / mass]


def quarter_stop(q):
    return min(D, (q + 1) * QUARTER)


def named_scratch(heads, tokens, vocab_rows):
    dma = pltpu.SemaphoreType.DMA
    rows = NX * NY * SLOTS
    stat = (8, rows // 2)
    width = heads * HD
    tiles = tokens // WINDOW
    lanes = heads * WINDOW
    return {
        "policy": pltpu.VMEM((vocab_rows, D), bf16),
        "frozen": pltpu.VMEM((vocab_rows, D), bf16),
        "proj": pltpu.VMEM((width, D), bf16),
        "key_cols": pltpu.VMEM((tokens, 128), bf16),
        "value_cols": pltpu.VMEM((tokens, 128), bf16),
        "kv_own": pltpu.VMEM((tokens, 128), bf16),
        "kv_halo": pltpu.VMEM((WINDOW, 128), bf16),
        "doc_own": pltpu.VMEM((8, WINDOW), f32),
        "doc_halo": pltpu.VMEM((8, WINDOW), f32),
        "key_ext": pltpu.VMEM((tokens + WINDOW, HD), bf16),
        "value_ext": pltpu.VMEM((tokens + WINDOW, HD), bf16),
        "key_marks": pltpu.VMEM((tiles + 1, WINDOW, WINDOW), f32),
        "query_t": pltpu.VMEM((width, tokens), bf16),
        "upper_t": pltpu.VMEM((width, tokens), f32),
        "prob": pltpu.VMEM((tiles, WINDOW, lanes), f32),
        "prob_low": pltpu.VMEM((tiles, 2 * WINDOW, lanes), bf16),
        "share": pltpu.VMEM((tiles, 1, lanes), f32),
        "attended": pltpu.VMEM((tiles, HD, lanes), f32),
        "query_grad": pltpu.VMEM((width, tokens), f32),
        "key_grad": pltpu.VMEM((HD, tokens + WINDOW), f32),
        "value_grad": pltpu.VMEM((HD, tokens + WINDOW), f32),
        "kv_send": pltpu.VMEM((2, HD // 2, tokens), bf16),
        "kv_recv": pltpu.VMEM((2, HD // 2, tokens), bf16),
        "edge_send": pltpu.VMEM((2, 2, HD // 2, WINDOW), bf16),
        "edge_recv": pltpu.VMEM((2, 2, HD // 2, WINDOW), bf16),
        "sink_y": pltpu.VMEM((NY, 8, WINDOW), f32),
        "sink_x": pltpu.VMEM((NX, 8, WINDOW), f32),
        "wide": pltpu.VMEM((4, SLOTS, QUARTER), f32),
        "gathered": pltpu.VMEM((2, NX, 2, PART, 2 * SLOTS, QUARTER), bf16),
        "rows": pltpu.VMEM((4, rows, QUARTER), bf16),
        "meta_y": pltpu.VMEM((NY,) + stat, f32),
        "meta_x": pltpu.VMEM((NX,) + stat, f32),
        "stat_xc": pltpu.VMEM((NX * NC,) + stat, f32),
        "stat_y": pltpu.VMEM((NY,) + stat, f32),
        "stat_z": pltpu.VMEM((NZ,) + stat, f32),
        "total": pltpu.VMEM((2, NX, NY * SLOTS, HALF), f32),
        "outgoing": pltpu.VMEM((NX, NY * SLOTS, HALF), bf16),
        "from_core": pltpu.VMEM((NX, NY * SLOTS, HALF), bf16),
        "send_x": pltpu.VMEM((NX, 2, PART * SLOTS, HALF), bf16),
        "relay": pltpu.VMEM((2, PART * SLOTS, HALF), bf16),
        "from_x": pltpu.VMEM((4, PART * SLOTS, HALF), bf16),
        "send_y": pltpu.VMEM((NY, 2 * SLOTS, QUARTER), bf16),
        "from_y": pltpu.VMEM((NY, 2 * SLOTS, QUARTER), bf16),
        "from_z": pltpu.VMEM((NZ, 2 * SLOTS, QUARTER), bf16),
        "final": pltpu.VMEM((2, 2 * SLOTS, QUARTER), f32),
        "load_sem": dma((5,)),
        "gy": dma((2, NY)),
        "gx": dma((2, 6)),
        "gc": dma((2, 8)),
        "my": dma((2, NY)),
        "mx": dma((2, NX)),
        "sxc": dma((2, NX * NC)),
        "sy": dma((2, NY)),
        "sz": dma((2, NZ)),
        "rc": dma((2, NX)),
        "rx": dma((2, 6)),
        "ry": dma((2, NY)),
        "rz": dma((2, NZ)),
        "fc": dma((2, 1)),
        "halo": dma((2, 2)),
        "kv": dma((2, 3)),
        "ky": dma((2, NY)),
        "kx": dma((2, NX)),
    }


class Names:
    def __init__(self, names, refs):
        for name, ref in zip(names, refs):
            setattr(self, name, ref)


def kernel_of(names):
    def kernel(*refs):
        policy_step(Names(names, refs))

    return kernel


def policy_step(r):
    seq, vocab = lax.axis_index("seq"), lax.axis_index("vocab")
    x, y = lax.rem(seq, NX), lax.div(seq, NX)
    z, c = lax.div(vocab, NC), lax.rem(vocab, NC)
    n_seq = NX * NY
    vocab_rows = r.policy.shape[0]
    tokens = r.queries.shape[0]
    heads = r.queries.shape[1] // HD
    tiles = tokens // WINDOW
    scale = HD ** (-0.5)
    left, right, far = wrap(x - 1, NX), wrap(x + 1, NX), wrap(x + 2, NX)
    y_part, y_sub = lax.div(y, PART), lax.rem(y, PART)

    def load(src, dst, k):
        copy = pltpu.make_async_copy(src, dst, r.load_sem.at[k])
        copy.start()
        return copy

    column = pl.multiple_of(lax.div(z, 2) * 128, 128)
    load_keys = load(r.keys_hbm.at[:, pl.ds(column, 128)], r.key_cols, 0)
    load_values = load(r.values_hbm.at[:, pl.ds(column, 128)], r.value_cols, 1)
    load_policy = load(r.policy_hbm, r.policy, 2)
    load_frozen = load(r.frozen_hbm, r.frozen, 3)
    load_proj = load(r.proj_hbm, r.proj, 4)

    def along_x(d, other=0):
        return device(wrap(x + d, NX), y, z, 1 - c if other else c)

    def along_y(d):
        return device(x, wrap(y + d, NY), z, c)

    def along_z(d):
        return device(x, y, wrap(z + d, NZ), c)

    across = device(x, y, z, 1 - c)
    to_right, to_left = along_x(1), along_x(-1)
    xc_steps = [(d, o) for d in range(NX) for o in range(NC) if d or o]
    prev, after = wrap(seq - 1, n_seq), wrap(seq + 1, n_seq)

    def send(src, dst, sems, k, target):
        copy = pltpu.make_async_remote_copy(
            src_ref=src,
            dst_ref=dst,
            send_sem=sems.at[0, k],
            recv_sem=sems.at[1, k],
            device_id=target,
            device_id_type=MESH,
        )
        copy.start()
        return copy

    def wait_all(copies):
        for copy in copies:
            copy.wait()

    barrier = pltpu.get_barrier_semaphore()
    peers = [along_x(d, o) for d, o in xc_steps]
    peers += [along_y(d) for d in range(1, NY)] + [along_z(d) for d in range(1, NZ)]
    peers += [(owner, z * NC + o) for owner in (prev, after) for o in range(NC)]
    for peer in peers:
        pl.semaphore_signal(barrier, inc=1, device_id=peer, device_id_type=MESH)

    hidden = r.hidden[...].astype(f32)
    r.wide[3] = jnp.zeros((SLOTS, QUARTER), f32)
    for q in range(4):
        r.wide[q, :, : quarter_stop(q) - q * QUARTER] = hidden[:, q * QUARTER : quarter_stop(q)]
    r.gathered[c, x, y_part, y_sub] = jnp.concatenate(
        [r.wide[2 * c], r.wide[2 * c + 1]], axis=0
    ).astype(bf16)
    stat = r.meta_y.shape[1:]
    field = lax.broadcasted_iota(jnp.int32, stat, 0)
    lane = lax.broadcasted_iota(jnp.int32, stat, 1) + jnp.where(field < 3, 0, stat[1])
    field = jnp.where(field < 3, field, field - 3)
    meta = jnp.zeros(stat, f32)
    first_lane = (x * NY + y) * SLOTS
    for k in range(SLOTS):
        values = [r.advantages[k], r.sampled[k].astype(f32), r.live[k].astype(f32)]
        value = jnp.where(field == 0, values[0], jnp.where(field == 1, values[1], values[2]))
        meta = jnp.where(lane == first_lane + k, value, meta)
    r.meta_y[y] = meta
    pl.semaphore_wait(barrier, len(peers))

    own_slot = r.gathered.at[c, x, y_part, y_sub]
    copies_y = [send(own_slot, own_slot, r.gy, d, along_y(d)) for d in range(1, NY)]
    metas_y = [send(r.meta_y.at[y], r.meta_y.at[y], r.my, d, along_y(d)) for d in range(1, NY)]

    load_keys.wait()
    load_values.wait()

    def swapped(block):
        return jnp.concatenate([block[:, HD:], block[:, :HD]], axis=1)

    key_cols, value_cols = r.key_cols[...].astype(f32), r.value_cols[...].astype(f32)
    even = lax.rem(z, 2) == 0
    key_part = jnp.where(even, key_cols, swapped(key_cols))
    value_part = jnp.where(even, swapped(value_cols), value_cols)
    low_lanes = lax.broadcasted_iota(jnp.int32, key_cols.shape, 1) < HD
    r.kv_own[...] = jnp.where(low_lanes, key_part, value_part).astype(bf16)
    docs = r.docs[...].astype(f32)
    r.doc_own[...] = jnp.broadcast_to(docs[tiles - 1 :], r.doc_own.shape)
    after_me = (after, vocab)
    halos = [
        send(r.kv_own.at[pl.ds(tokens - WINDOW, WINDOW)], r.kv_halo, r.halo, 0, after_me),
        send(r.doc_own, r.doc_halo, r.halo, 1, after_me),
    ]
    r.query_t[...] = jnp.transpose(r.queries[...].astype(f32)).astype(bf16)
    r.upper_t[...] = jnp.transpose(r.upper[...].astype(f32))

    key_row = lax.broadcasted_iota(jnp.int32, (WINDOW, WINDOW), 0)
    query_col = lax.broadcasted_iota(jnp.int32, (WINDOW, WINDOW), 1)
    earlier = key_row > query_col

    def per_head(block):
        return jnp.concatenate([block] * heads, axis=1)

    def by_head(ref, t):
        lanes = slice(t * WINDOW, (t + 1) * WINDOW)
        return jnp.concatenate([ref[h * HD : (h + 1) * HD, lanes] for h in range(heads)], axis=1)

    earlier_wide = per_head(earlier.astype(f32)) > 0.5
    sink_row = jnp.concatenate([jnp.full((1, WINDOW), r.sinks[h]) for h in range(heads)], axis=1)

    def both_blocks(block):
        return jnp.concatenate(
            [jnp.where(earlier_wide, block, 0.0), jnp.where(earlier_wide, 0.0, block)], axis=0
        ).astype(bf16)

    def one_block(strip):
        return jnp.where(earlier_wide, strip[:WINDOW], strip[WINDOW:])

    def attention_setup():
        wait_all(halos)
        kv_halo = r.kv_halo[...].astype(f32)
        kv_own = r.kv_own[...].astype(f32)
        r.key_ext[:WINDOW] = kv_halo[:, :HD].astype(bf16)
        r.key_ext[WINDOW:] = kv_own[:, :HD].astype(bf16)
        r.value_ext[:WINDOW] = kv_halo[:, HD:].astype(bf16)
        r.value_ext[WINDOW:] = kv_own[:, HD:].astype(bf16)
        halo_docs = jnp.where(seq == 0, -1.0, r.doc_halo[0:1])
        for t in range(tiles + 1):
            row = halo_docs if t == 0 else docs[t - 1 : t]
            r.key_marks[t] = jnp.transpose(jnp.broadcast_to(row, (WINDOW, WINDOW)))

    def attention_forward(t):
        strip = slice(t * WINDOW, (t + 2) * WINDOW)
        marks = jnp.where(earlier, r.key_marks[t], r.key_marks[t + 1])
        allowed = per_head((marks == docs[t : t + 1]).astype(f32)) > 0.5
        scores = one_block(
            jnp.dot(r.key_ext[strip], by_head(r.query_t, t), preferred_element_type=f32)
        )
        masked = jnp.where(allowed, scores * scale, masked_score)
        row_top = jnp.maximum(jnp.max(masked, axis=0, keepdims=True), sink_row)
        exp_terms = jnp.where(allowed, jnp.exp(masked - row_top), 0.0)
        sink_term = jnp.exp(sink_row - row_top)
        inverse = 1.0 / (jnp.sum(exp_terms, axis=0, keepdims=True) + sink_term)
        prob = exp_terms * inverse
        low = both_blocks(prob)
        r.prob[t] = prob
        r.prob_low[t] = low
        r.share[t] = sink_term * inverse
        r.attended[t] = lax.dot_general(
            r.value_ext[strip], low, contract_first, preferred_element_type=f32
        )

    wait_all(copies_y)
    sent_x = [
        send(r.gathered.at[c, x, part], r.gathered.at[c, x, part], r.gx, k, target)
        for k, (part, target) in enumerate(
            [(0, to_right), (1, to_left), (1, to_right), (0, to_left)]
        )
    ]
    sent_c = []

    def cross_send(group, part):
        block = r.gathered.at[c, group, part]
        sent_c.append(send(block, block, r.gc, len(sent_c), across))

    def arrange(half, group, part):
        block = r.gathered[half, group, part].astype(f32).reshape(PART, 2, SLOTS, QUARTER)
        start = pl.multiple_of((group * 2 + part) * (PART * SLOTS), PART * SLOTS)
        for k in range(2):
            r.rows[2 * half + k, pl.ds(start, PART * SLOTS), :] = (
                block[:, k].reshape(PART * SLOTS, QUARTER).astype(bf16)
            )

    cross_send(x, 0)
    cross_send(x, 1)
    wait_all(metas_y)
    meta = r.meta_y[0]
    for k in range(1, NY):
        meta += r.meta_y[k]
    r.meta_x[x] = meta
    metas_x = [send(r.meta_x.at[x], r.meta_x.at[x], r.mx, d, along_x(d)) for d in range(1, NX)]
    attention_setup()
    sent_x[0].wait_recv()
    sent_x.append(
        send(r.gathered.at[c, left, 0], r.gathered.at[c, left, 0], r.gx, 4, to_right)
    )
    cross_send(left, 0)
    sent_x[1].wait_recv()
    sent_x.append(
        send(r.gathered.at[c, right, 1], r.gathered.at[c, right, 1], r.gx, 5, to_left)
    )
    cross_send(right, 1)
    arrange(c, x, 0)
    arrange(c, x, 1)
    attention_forward(0)
    sent_x[2].wait_recv()
    cross_send(left, 1)
    sent_x[3].wait_recv()
    cross_send(right, 0)
    arrange(c, left, 0)
    arrange(c, right, 1)
    for t in range(1, tiles):
        attention_forward(t)
    sent_x[4].wait_recv()
    cross_send(far, 0)
    sent_x[5].wait_recv()
    cross_send(far, 1)
    arrange(c, left, 1)
    arrange(c, right, 0)
    arrange(c, far, 0)
    arrange(c, far, 1)
    order = [(x, 0), (x, 1), (left, 0), (right, 1), (left, 1), (right, 0), (far, 0), (far, 1)]
    for copy, (group, part) in zip(sent_c, order):
        copy.wait_recv()
        arrange(1 - c, group, part)
    for copy in sent_x + sent_c:
        copy.wait_send()
    wait_all(metas_x)
    meta = r.meta_x[0]
    for k in range(1, NX):
        meta += r.meta_x[k]

    load_policy.wait()
    load_frozen.wait()

    def logits_of(head):
        result = 0.0
        for q in range(4):
            stop = quarter_stop(q)
            result += lax.dot_general(
                head[:, q * QUARTER : stop],
                r.rows[q, :, : stop - q * QUARTER],
                contract_last,
                preferred_element_type=f32,
            )
        return result

    policy_logits = logits_of(r.policy)
    frozen_logits = logits_of(r.frozen)
    policy_peak = jnp.max(policy_logits, axis=0, keepdims=True)
    frozen_peak = jnp.max(frozen_logits, axis=0, keepdims=True)
    logit_diff = policy_logits - frozen_logits
    policy_terms = jnp.exp(policy_logits - policy_peak)
    mass = jnp.sum(policy_terms, axis=0, keepdims=True)
    mean = jnp.sum(policy_terms * logit_diff, axis=0, keepdims=True) / mass
    frozen_mass = jnp.sum(jnp.exp(frozen_logits - frozen_peak), axis=0, keepdims=True)
    stats = [policy_peak + jnp.log(mass), frozen_peak + jnp.log(frozen_mass), mean]

    r.stat_xc[0] = fold(stats)
    wait_all(
        [
            send(r.stat_xc.at[0], r.stat_xc.at[k + 1], r.sxc, k, along_x(d, o))
            for k, (d, o) in enumerate(xc_steps)
        ]
    )
    r.stat_y[0] = fold(merged([r.stat_xc[k] for k in range(NX * NC)]))
    wait_all([send(r.stat_y.at[0], r.stat_y.at[d], r.sy, d, along_y(d)) for d in range(1, NY)])
    r.stat_z[0] = fold(merged([r.stat_y[k] for k in range(NY)]))
    wait_all([send(r.stat_z.at[0], r.stat_z.at[d], r.sz, d, along_z(d)) for d in range(1, NZ)])
    policy_lognorm, frozen_lognorm, cross_total = merged([r.stat_z[k] for k in range(NZ)])

    divergence = cross_total - policy_lognorm + frozen_lognorm
    policy_prob = jnp.exp(policy_logits - policy_lognorm)
    first_id = (seq * (NZ * NC) + vocab) * vocab_rows
    ids_here = (first_id + lax.broadcasted_iota(jnp.int32, policy_logits.shape, 0)).astype(f32)
    picked = (ids_here == unfold(meta, 1)).astype(f32)
    weight = loss_scale * unfold(meta, 2)
    log_ratio = policy_logits - policy_lognorm - (frozen_logits - frozen_lognorm) - divergence
    logit_grad = (
        weight * (-unfold(meta, 0) * (picked - policy_prob) + kl_weight * policy_prob * log_ratio)
    ).astype(bf16)

    group_rows = NY * SLOTS
    r.total[1, :, :, QUARTER:] = jnp.zeros((NX, group_rows, QUARTER), f32)
    for q in range(4):
        stop = quarter_stop(q)
        half, low = q // 2, (q % 2) * QUARTER
        r.total[half, :, :, low : low + stop - q * QUARTER] = lax.dot_general(
            logit_grad, r.policy[:, q * QUARTER : stop], contract_first, preferred_element_type=f32
        ).reshape(NX, group_rows, stop - q * QUARTER)
    cores = []
    for k, group in enumerate([far, right, left, x]):
        r.outgoing[group] = r.total[1 - c, group].astype(bf16)
        cores.append(send(r.outgoing.at[group], r.from_core.at[group], r.rc, k, across))
    part_rows = PART * SLOTS
    low_part, high_part = slice(0, part_rows), slice(part_rows, 2 * part_rows)

    def chip_sum(k, group):
        cores[k].wait_recv()
        return r.total[c, group] + r.from_core[group].astype(f32)

    both = chip_sum(0, far)
    r.send_x[far, 0] = both[low_part].astype(bf16)
    r.send_x[far, 1] = both[high_part].astype(bf16)
    reduced = [
        send(r.send_x.at[far, 0], r.relay.at[0], r.rx, 0, to_right),
        send(r.send_x.at[far, 1], r.relay.at[1], r.rx, 1, to_left),
    ]
    for_right = chip_sum(1, right)
    r.send_x[right, 1] = for_right[high_part].astype(bf16)
    reduced.append(send(r.send_x.at[right, 1], r.from_x.at[0], r.rx, 2, to_right))
    r.total[c, right, low_part] = for_right[low_part]
    for_left = chip_sum(2, left)
    r.send_x[left, 0] = for_left[low_part].astype(bf16)
    reduced.append(send(r.send_x.at[left, 0], r.from_x.at[1], r.rx, 3, to_left))
    r.total[c, left, high_part] = for_left[high_part]
    reduced[0].wait_recv()
    r.send_x[right, 0] = (r.total[c, right, low_part] + r.relay[0].astype(f32)).astype(bf16)
    reduced.append(send(r.send_x.at[right, 0], r.from_x.at[2], r.rx, 4, to_right))
    reduced[1].wait_recv()
    r.send_x[left, 1] = (r.total[c, left, high_part] + r.relay[1].astype(f32)).astype(bf16)
    reduced.append(send(r.send_x.at[left, 1], r.from_x.at[3], r.rx, 5, to_left))
    r.total[c, x] = chip_sum(3, x)
    for copy in reduced[2:]:
        copy.wait_recv()
    pairs = [(low_part, 1, 2), (high_part, 0, 3)]
    for part, (rows, first, second) in enumerate(pairs):
        mine = r.total[c, x, rows] + r.from_x[first].astype(f32) + r.from_x[second].astype(f32)
        mine = mine.reshape(PART, SLOTS, HALF)
        packed = jnp.concatenate([mine[:, :, :QUARTER], mine[:, :, QUARTER:]], axis=1)
        r.send_y[part * PART : (part + 1) * PART] = packed.astype(bf16)
    copies = [
        send(r.send_y.at[wrap(y + d, NY)], r.from_y.at[d], r.ry, d, along_y(d))
        for d in range(1, NY)
    ]
    for copy in cores + reduced:
        copy.wait_send()
    wait_all(copies)
    summed = r.send_y[y].astype(f32)
    for k in range(1, NY):
        summed += r.from_y[k].astype(f32)
    r.from_z[z] = summed.astype(bf16)
    wait_all([send(r.from_z.at[z], r.from_z.at[z], r.rz, d, along_z(d)) for d in range(1, NZ)])
    summed = r.from_z[0].astype(f32)
    for k in range(1, NZ):
        summed += r.from_z[k].astype(f32)
    r.final[c] = summed
    copy = send(r.final.at[c], r.final.at[c], r.fc, 0, across)
    load_proj.wait()
    copy.wait()

    slot_grad = 0.0
    for q in range(4):
        stop = quarter_stop(q)
        part = r.final[q // 2, (q % 2) * SLOTS : (q % 2 + 1) * SLOTS, :][:, : stop - q * QUARTER]
        r.hidden_grad[:, q * QUARTER : stop] = part
        slot_grad += lax.dot_general(
            r.proj[:, q * QUARTER : stop],
            part.astype(bf16),
            contract_last,
            preferred_element_type=f32,
        )
    slot_row = lax.broadcasted_iota(jnp.int32, (SLOTS, tokens), 0)
    token = lax.broadcasted_iota(jnp.int32, (SLOTS, tokens), 1)
    landing = jnp.zeros((SLOTS, tokens), f32)
    for k in range(SLOTS):
        landing = jnp.where((slot_row == k) & (token == r.slot_pos[k]), 1.0, landing)
    added = jnp.dot(slot_grad, landing, preferred_element_type=f32)
    r.upper_t[...] = (r.upper_t[...] + added).astype(bf16).astype(f32)

    deltas = []
    sink_total = 0.0
    for t in range(tiles):
        delta = jnp.sum(by_head(r.upper_t, t) * r.attended[t], axis=0, keepdims=True)
        deltas.append(delta)
        sink_total += r.share[t] * delta
    sink_rows = [-sink_total[:, h * WINDOW : (h + 1) * WINDOW] for h in range(heads)]
    sink_rows.append(jnp.zeros((8 - heads, WINDOW), f32))
    r.sink_y[y] = jnp.concatenate(sink_rows, axis=0)
    sinks_y = [send(r.sink_y.at[y], r.sink_y.at[y], r.ky, d, along_y(d)) for d in range(1, NY)]

    r.key_grad[...] = jnp.zeros(r.key_grad.shape, f32)
    r.value_grad[...] = jnp.zeros(r.value_grad.shape, f32)
    for t in range(tiles):
        strip = slice(t * WINDOW, (t + 2) * WINDOW)
        grads = by_head(r.upper_t, t).astype(bf16)
        dprob = one_block(jnp.dot(r.value_ext[strip], grads, preferred_element_type=f32))
        dscore = both_blocks(r.prob[t] * (dprob - deltas[t]))
        r.key_grad[:, strip] += lax.dot_general(
            by_head(r.query_t, t), dscore, contract_last, preferred_element_type=f32
        )
        r.value_grad[:, strip] += lax.dot_general(
            grads, r.prob_low[t], contract_last, preferred_element_type=f32
        )
        query_grad = scale * lax.dot_general(
            r.key_ext[strip], dscore, contract_first, preferred_element_type=f32
        )
        for h in range(heads):
            r.query_grad[h * HD : (h + 1) * HD, t * WINDOW : (t + 1) * WINDOW] = query_grad[
                :, h * WINDOW : (h + 1) * WINDOW
            ]
    half_width = HD // 2
    mine_rows = pl.ds(pl.multiple_of(c * half_width, half_width), half_width)
    other_rows = pl.ds(pl.multiple_of((1 - c) * half_width, half_width), half_width)
    both_grads = [(r.key_grad, scale), (r.value_grad, 1.0)]
    for k, (grad, factor) in enumerate(both_grads):
        r.kv_send[k] = (grad[other_rows, WINDOW:] * factor).astype(bf16)
        r.edge_send[0, k] = (grad[mine_rows, :WINDOW] * factor).astype(bf16)
        r.edge_send[1, k] = (grad[other_rows, :WINDOW] * factor).astype(bf16)
    kv_copies = [
        send(r.edge_send.at[0], r.edge_recv.at[0], r.kv, 0, (prev, vocab)),
        send(r.edge_send.at[1], r.edge_recv.at[1], r.kv, 1, (prev, z * NC + 1 - c)),
        send(r.kv_send, r.kv_recv, r.kv, 2, across),
    ]
    wait_all(sinks_y)
    sink_sum = r.sink_y[0]
    for k in range(1, NY):
        sink_sum += r.sink_y[k]
    r.sink_x[x] = sink_sum
    sinks_x = [send(r.sink_x.at[x], r.sink_x.at[x], r.kx, d, along_x(d)) for d in range(1, NX)]
    r.grad_queries[...] = jnp.transpose(r.query_grad[...]).astype(bf16)
    wait_all(kv_copies)
    for k, (grad, factor) in enumerate(both_grads):
        own = grad[mine_rows, WINDOW:] * factor + r.kv_recv[k].astype(f32)
        edge = r.edge_recv[0, k].astype(f32) + r.edge_recv[1, k].astype(f32)
        r.grad_kv[k] = jnp.concatenate(
            [own[:, : tokens - WINDOW], own[:, tokens - WINDOW :] + edge], axis=1
        ).astype(bf16)
    wait_all(sinks_x)
    sink_sum = r.sink_x[0]
    for k in range(1, NX):
        sink_sum += r.sink_x[k]
    r.grad_sinks[...] = jnp.broadcast_to(jnp.sum(sink_sum, axis=1, keepdims=True), (8, WINDOW))


def shards(
    queries,
    keys,
    values,
    sinks,
    doc_ids,
    upper_grad,
    out_proj,
    final_hidden,
    advantages,
    slot_pos,
    slot_live,
    sampled_ids,
    policy_head,
    reference_head,
):
    vmem = pl.BlockSpec(memory_space=pltpu.VMEM)
    smem = pl.BlockSpec(memory_space=pltpu.SMEM)
    hbm = pl.BlockSpec(memory_space=pl.ANY)
    heads = sinks.shape[0]
    tokens = queries.shape[0]
    operands = [
        ("hidden", final_hidden, vmem),
        ("advantages", advantages.astype(f32), smem),
        ("sampled", sampled_ids, smem),
        ("live", slot_live, smem),
        ("slot_pos", slot_pos, smem),
        ("sinks", sinks, smem),
        ("queries", queries, vmem),
        ("upper", upper_grad, vmem),
        ("docs", doc_ids.reshape(tokens // WINDOW, WINDOW), vmem),
        ("keys_hbm", keys, hbm),
        ("values_hbm", values, hbm),
        ("proj_hbm", out_proj, hbm),
        ("policy_hbm", policy_head, hbm),
        ("frozen_hbm", reference_head, hbm),
    ]
    results = [
        ("grad_queries", jax.ShapeDtypeStruct(queries.shape, bf16)),
        ("grad_kv", jax.ShapeDtypeStruct((2, HD // 2, tokens), bf16)),
        ("grad_sinks", jax.ShapeDtypeStruct((8, WINDOW), f32)),
        ("hidden_grad", jax.ShapeDtypeStruct(final_hidden.shape, f32)),
    ]
    scratch = named_scratch(heads, tokens, policy_head.shape[0])
    names = [name for name, _, _ in operands] + [name for name, _ in results] + list(scratch)
    grad_queries, grad_kv, grad_sinks, hidden_grad = pl.pallas_call(
        kernel_of(names),
        out_shape=[shape for _, shape in results],
        in_specs=[spec for _, _, spec in operands],
        out_specs=[vmem] * len(results),
        scratch_shapes=list(scratch.values()),
        compiler_params=pltpu.CompilerParams(
            collective_id=0, has_side_effects=True, vmem_limit_bytes=56 * 2**20
        ),
    )(*[value for _, value, _ in operands])
    return (grad_queries, grad_kv, grad_sinks[:heads, 0], hidden_grad)


def solution(mesh):
    in_specs = (
        P("seq", "vocab"),
        P("seq", None),
        P("seq", None),
        P("vocab"),
        P("seq"),
        P("seq", "vocab"),
        P("vocab", None),
        P("seq", None),
        P("seq"),
        P("seq"),
        P("seq"),
        P("seq"),
        P(("seq", "vocab"), None),
        P(("seq", "vocab"), None),
    )
    out_specs = (P("seq", "vocab"), P(None, "vocab", "seq"), P("vocab"), P("seq", None))
    return jax.shard_map(shards, mesh=mesh, in_specs=in_specs, out_specs=out_specs, check_vma=False)
```

time: 631 us -> 96.3 us (0.15)
  the two profiles are of different devices: /device:TPU:32 before, /device:TPU:1 now
where the time goes in v2:
time: 96.3 us; the launch traced here: 95.9 us
  Pallas kernels  85.6 us (89%)
  local copies, waits for them, and re-layouts  8.54 us (9%)
  other arithmetic  1.17 us (1%)
    pallas_call x1, Pallas kernels, shards(): pl.pallas_call(kernel_of(names), out_shape=[shape for _, shape in results...  85.6 us
    unnamed x4, local copies, waits for them, and re-layouts  7.24 us

profile of v2, /device:TPU:1, one launch (start us, length us, event | category | flops | bytes accessed | tf_op | source)
XLA Modules:
  0.0 95.9 jit_solution(1480396682001249594)
XLA Ops:
  0.6 1.2 %convert_element_type.3.refs_1_ = f32[8]{0:T(128)} convert(bf16[8]{0:T(256)(128)(2,1)} %param.22) | non-fusion elementwise | flops 8 | bytes 48 | tf_op jit(solution)/shard_map/convert_element_type | solution.py:611
  1.8 2.6 %copy.19.refs_11_ = bf16[256,2880]{1,0:T(8,128)(2,1)} copy(bf16[256,2880]{0,1:T(8,128)(2,1)} %param.20) | data formatting | bytes 2949120 | tf_op args[6]
  4.4 85.6 %shard_map.165 = (bf16[512,256]{1,0:T(8,128)(2,1)}, bf16[2,32,512]{2,1,0:T(8,128)(2,1)}, f32[8,128]{1,0:T(8,128)}, f32[8,2880]{1,0:T(8,128)}) custom-call(bf16[8,2880]{1,0:T(8,128)(2,1)} %refs_0_.1, f32[8]{0:T(128)} %convert_element_type.3.refs_1_, s32[8]{0:T(128)} %refs_2_.1, s32[8]{0:T(128)} %refs_3_.1, s32[8]{0:T(128)} %refs_4_.1, f32[4]{0:T(128)} %refs_5_.1, ...), custom_call_target="tpu_custom_call" | custom-call | tf_op jit(solution)/shard_map/pallas_call | solution.py:633
  90.0 1.3 %slice_reduce_fusion = f32[4]{0:T(128)} fusion(f32[8,128]{1,0:T(8,128)} %get-tuple-element.10), kind=kLoop, calls=%fused_computation | loop fusion | bytes 32 | tf_op jit(solution)/shard_map/slice | solution.py:643
  91.3 1.7 %copy.23 = bf16[512,256]{1,0:T(8,128)(2,1)} copy(bf16[512,256]{1,0:T(8,128)(2,1)} %get-tuple-element.16) | data formatting | bytes 524288
  92.9 1.5 %copy.24 = bf16[2,32,512]{2,1,0:T(8,128)(2,1)} copy(bf16[2,32,512]{2,1,0:T(8,128)(2,1)} %get-tuple-element.17) | data formatting | bytes 131072
  94.4 1.5 %copy.25 = f32[8,2880]{1,0:T(8,128)} copy(f32[8,2880]{1,0:T(8,128)} %get-tuple-element.19) | data formatting | bytes 184320

commit v3 on v2

--- a/solution.py
+++ b/solution.py
@@ -13,6 +13,7 @@
 HALF = 2 * QUARTER
 SLOTS = 8
 PART = NY // 2
+CHUNK = QUARTER // 2
 
 loss_scale = 64.0
 kl_weight = 1.0
@@ -57,6 +58,10 @@
     return [tops[0] + jnp.log(mass), tops[1] + jnp.log(frozen), cross / mass]
 
 
+def far_first(size):
+    return sorted(range(1, size), key=lambda d: (-min(d, size - d), d))
+
+
 def quarter_stop(q):
     return min(D, (q + 1) * QUARTER)
 
@@ -71,7 +76,7 @@
     return {
         "policy": pltpu.VMEM((vocab_rows, D), bf16),
         "frozen": pltpu.VMEM((vocab_rows, D), bf16),
-        "proj": pltpu.VMEM((width, D), bf16),
+        "proj": pltpu.VMEM((D, width), bf16),
         "key_cols": pltpu.VMEM((tokens, 128), bf16),
         "value_cols": pltpu.VMEM((tokens, 128), bf16),
         "kv_own": pltpu.VMEM((tokens, 128), bf16),
@@ -97,37 +102,40 @@
         "sink_y": pltpu.VMEM((NY, 8, WINDOW), f32),
         "sink_x": pltpu.VMEM((NX, 8, WINDOW), f32),
         "wide": pltpu.VMEM((4, SLOTS, QUARTER), f32),
-        "gathered": pltpu.VMEM((2, NX, 2, PART, 2 * SLOTS, QUARTER), bf16),
+        "gathered": pltpu.VMEM((2, 2, NX, 2, PART, 2 * SLOTS, CHUNK), bf16),
         "rows": pltpu.VMEM((4, rows, QUARTER), bf16),
         "meta_y": pltpu.VMEM((NY,) + stat, f32),
         "meta_x": pltpu.VMEM((NX,) + stat, f32),
         "stat_xc": pltpu.VMEM((NX * NC,) + stat, f32),
         "stat_y": pltpu.VMEM((NY,) + stat, f32),
         "stat_z": pltpu.VMEM((NZ,) + stat, f32),
-        "total": pltpu.VMEM((2, NX, NY * SLOTS, HALF), f32),
-        "outgoing": pltpu.VMEM((NX, NY * SLOTS, HALF), bf16),
-        "from_core": pltpu.VMEM((NX, NY * SLOTS, HALF), bf16),
-        "send_x": pltpu.VMEM((NX, 2, PART * SLOTS, HALF), bf16),
-        "relay": pltpu.VMEM((2, PART * SLOTS, HALF), bf16),
-        "from_x": pltpu.VMEM((4, PART * SLOTS, HALF), bf16),
-        "send_y": pltpu.VMEM((NY, 2 * SLOTS, QUARTER), bf16),
-        "from_y": pltpu.VMEM((NY, 2 * SLOTS, QUARTER), bf16),
-        "from_z": pltpu.VMEM((NZ, 2 * SLOTS, QUARTER), bf16),
-        "final": pltpu.VMEM((2, 2 * SLOTS, QUARTER), f32),
-        "load_sem": dma((5,)),
-        "gy": dma((2, NY)),
-        "gx": dma((2, 6)),
-        "gc": dma((2, 8)),
+        "total": pltpu.VMEM((4, NX, NY * SLOTS, QUARTER), f32),
+        "outgoing": pltpu.VMEM((2, NX, NY * SLOTS, QUARTER), bf16),
+        "from_core": pltpu.VMEM((2, NX, NY * SLOTS, QUARTER), bf16),
+        "send_x": pltpu.VMEM((2, NX, 2, PART * SLOTS, QUARTER), bf16),
+        "relay": pltpu.VMEM((2, 2, PART * SLOTS, QUARTER), bf16),
+        "from_x": pltpu.VMEM((2, 4, PART * SLOTS, QUARTER), bf16),
+        "send_y": pltpu.VMEM((2, NY, 2 * SLOTS, CHUNK), bf16),
+        "from_y": pltpu.VMEM((2, NY, 2 * SLOTS, CHUNK), bf16),
+        "from_z": pltpu.VMEM((2, NZ, 2 * SLOTS, CHUNK), bf16),
+        "final": pltpu.VMEM((4, 2 * SLOTS, CHUNK), f32),
+        "queries": pltpu.VMEM((tokens, width), bf16),
+        "upper": pltpu.VMEM((tokens, width), bf16),
+        "dscore": pltpu.VMEM((tiles, 2 * WINDOW, lanes), bf16),
+        "load_sem": dma((7,)),
+        "gy": dma((2, 2 * NY)),
+        "gx": dma((2, 12)),
+        "gc": dma((2, 16)),
         "my": dma((2, NY)),
         "mx": dma((2, NX)),
         "sxc": dma((2, NX * NC)),
         "sy": dma((2, NY)),
         "sz": dma((2, NZ)),
-        "rc": dma((2, NX)),
-        "rx": dma((2, 6)),
-        "ry": dma((2, NY)),
-        "rz": dma((2, NZ)),
-        "fc": dma((2, 1)),
+        "rc": dma((2, 2 * NX)),
+        "rx": dma((2, 12)),
+        "ry": dma((2, 2 * NY)),
+        "rz": dma((2, 2 * NZ)),
+        "fc": dma((2, 2)),
         "halo": dma((2, 2)),
         "kv": dma((2, 3)),
         "ky": dma((2, NY)),
@@ -172,6 +180,8 @@
     load_policy = load(r.policy_hbm, r.policy, 2)
     load_frozen = load(r.frozen_hbm, r.frozen, 3)
     load_proj = load(r.proj_hbm, r.proj, 4)
+    load_queries = load(r.queries_hbm, r.queries, 5)
+    load_upper = load(r.upper_hbm, r.upper, 6)
 
     def along_x(d, other=0):
         return device(wrap(x + d, NX), y, z, 1 - c if other else c)
@@ -214,9 +224,9 @@
     r.wide[3] = jnp.zeros((SLOTS, QUARTER), f32)
     for q in range(4):
         r.wide[q, :, : quarter_stop(q) - q * QUARTER] = hidden[:, q * QUARTER : quarter_stop(q)]
-    r.gathered[c, x, y_part, y_sub] = jnp.concatenate(
-        [r.wide[2 * c], r.wide[2 * c + 1]], axis=0
-    ).astype(bf16)
+    packed = jnp.concatenate([r.wide[2 * c], r.wide[2 * c + 1]], axis=0).astype(bf16)
+    for k in range(2):
+        r.gathered[k, c, x, y_part, y_sub] = packed[:, k * CHUNK : (k + 1) * CHUNK]
     stat = r.meta_y.shape[1:]
     field = lax.broadcasted_iota(jnp.int32, stat, 0)
     lane = lax.broadcasted_iota(jnp.int32, stat, 1) + jnp.where(field < 3, 0, stat[1])
@@ -224,14 +234,19 @@
     meta = jnp.zeros(stat, f32)
     first_lane = (x * NY + y) * SLOTS
     for k in range(SLOTS):
-        values = [r.advantages[k], r.sampled[k].astype(f32), r.live[k].astype(f32)]
-        value = jnp.where(field == 0, values[0], jnp.where(field == 1, values[1], values[2]))
+        value = jnp.where(field == 1, r.sampled[k].astype(f32), r.live[k].astype(f32))
         meta = jnp.where(lane == first_lane + k, value, meta)
+    advantages = jnp.concatenate([r.advantages[...].astype(f32)] * (stat[1] // SLOTS), axis=1)
+    mine_here = (lane >= first_lane) & (lane < first_lane + SLOTS) & (field == 0)
+    meta = jnp.where(mine_here, jnp.broadcast_to(advantages, stat), meta)
     r.meta_y[y] = meta
     pl.semaphore_wait(barrier, len(peers))
 
-    own_slot = r.gathered.at[c, x, y_part, y_sub]
-    copies_y = [send(own_slot, own_slot, r.gy, d, along_y(d)) for d in range(1, NY)]
+    copies_y = [[], []]
+    for k in range(2):
+        own_slot = r.gathered.at[k, c, x, y_part, y_sub]
+        for d in far_first(NY):
+            copies_y[k].append(send(own_slot, own_slot, r.gy, k * NY + d, along_y(d)))
     metas_y = [send(r.meta_y.at[y], r.meta_y.at[y], r.my, d, along_y(d)) for d in range(1, NY)]
 
     load_keys.wait()
@@ -253,6 +268,8 @@
         send(r.kv_own.at[pl.ds(tokens - WINDOW, WINDOW)], r.kv_halo, r.halo, 0, after_me),
         send(r.doc_own, r.doc_halo, r.halo, 1, after_me),
     ]
+    load_queries.wait()
+    load_upper.wait()
     r.query_t[...] = jnp.transpose(r.queries[...].astype(f32)).astype(bf16)
     r.upper_t[...] = jnp.transpose(r.upper[...].astype(f32))
 
@@ -312,29 +329,59 @@
             r.value_ext[strip], low, contract_first, preferred_element_type=f32
         )
 
-    wait_all(copies_y)
-    sent_x = [
-        send(r.gathered.at[c, x, part], r.gathered.at[c, x, part], r.gx, k, target)
-        for k, (part, target) in enumerate(
-            [(0, to_right), (1, to_left), (1, to_right), (0, to_left)]
-        )
-    ]
-    sent_c = []
-
-    def cross_send(group, part):
-        block = r.gathered.at[c, group, part]
-        sent_c.append(send(block, block, r.gc, len(sent_c), across))
-
-    def arrange(half, group, part):
-        block = r.gathered[half, group, part].astype(f32).reshape(PART, 2, SLOTS, QUARTER)
+    sent_x, sent_c, order = [[], []], [[], []], [[], []]
+
+    def along(k, group, part, target):
+        block = r.gathered.at[k, c, group, part]
+        sent_x[k].append(send(block, block, r.gx, 6 * k + len(sent_x[k]), target))
+
+    def cross_send(k, group, part):
+        block = r.gathered.at[k, c, group, part]
+        sent_c[k].append(send(block, block, r.gc, 8 * k + len(sent_c[k]), across))
+        order[k].append((group, part))
+
+    def arrange(k, half, group, part):
+        block = r.gathered[k, half, group, part].astype(f32).reshape(PART, 2, SLOTS, CHUNK)
         start = pl.multiple_of((group * 2 + part) * (PART * SLOTS), PART * SLOTS)
-        for k in range(2):
-            r.rows[2 * half + k, pl.ds(start, PART * SLOTS), :] = (
-                block[:, k].reshape(PART * SLOTS, QUARTER).astype(bf16)
-            )
-
-    cross_send(x, 0)
-    cross_send(x, 1)
+        for low in range(2):
+            r.rows[
+                2 * half + low, pl.ds(start, PART * SLOTS), k * CHUNK : (k + 1) * CHUNK
+            ] = block[:, low].reshape(PART * SLOTS, CHUNK).astype(bf16)
+
+    def spread(k):
+        wait_all(copies_y[k])
+        along(k, x, 0, to_right)
+        along(k, x, 1, to_left)
+        along(k, x, 1, to_right)
+        along(k, x, 0, to_left)
+        cross_send(k, x, 0)
+        cross_send(k, x, 1)
+
+    def relay_on(k):
+        sent_x[k][0].wait_recv()
+        along(k, left, 0, to_right)
+        cross_send(k, left, 0)
+        sent_x[k][1].wait_recv()
+        along(k, right, 1, to_left)
+        cross_send(k, right, 1)
+
+    def direct_rest(k):
+        sent_x[k][2].wait_recv()
+        cross_send(k, left, 1)
+        sent_x[k][3].wait_recv()
+        cross_send(k, right, 0)
+
+    def far_rest(k):
+        sent_x[k][4].wait_recv()
+        cross_send(k, far, 0)
+        sent_x[k][5].wait_recv()
+        cross_send(k, far, 1)
+
+    def arrange_own(k):
+        for group, part in order[k]:
+            arrange(k, c, group, part)
+
+    spread(0)
     wait_all(metas_y)
     meta = r.meta_y[0]
     for k in range(1, NY):
@@ -342,40 +389,25 @@
     r.meta_x[x] = meta
     metas_x = [send(r.meta_x.at[x], r.meta_x.at[x], r.mx, d, along_x(d)) for d in range(1, NX)]
     attention_setup()
-    sent_x[0].wait_recv()
-    sent_x.append(
-        send(r.gathered.at[c, left, 0], r.gathered.at[c, left, 0], r.gx, 4, to_right)
-    )
-    cross_send(left, 0)
-    sent_x[1].wait_recv()
-    sent_x.append(
-        send(r.gathered.at[c, right, 1], r.gathered.at[c, right, 1], r.gx, 5, to_left)
-    )
-    cross_send(right, 1)
-    arrange(c, x, 0)
-    arrange(c, x, 1)
+    spread(1)
+    relay_on(0)
     attention_forward(0)
-    sent_x[2].wait_recv()
-    cross_send(left, 1)
-    sent_x[3].wait_recv()
-    cross_send(right, 0)
-    arrange(c, left, 0)
-    arrange(c, right, 1)
-    for t in range(1, tiles):
+    relay_on(1)
+    direct_rest(0)
+    attention_forward(1)
+    direct_rest(1)
+    far_rest(0)
+    attention_forward(2)
+    arrange_own(0)
+    far_rest(1)
+    for t in range(3, tiles):
         attention_forward(t)
-    sent_x[4].wait_recv()
-    cross_send(far, 0)
-    sent_x[5].wait_recv()
-    cross_send(far, 1)
-    arrange(c, left, 1)
-    arrange(c, right, 0)
-    arrange(c, far, 0)
-    arrange(c, far, 1)
-    order = [(x, 0), (x, 1), (left, 0), (right, 1), (left, 1), (right, 0), (far, 0), (far, 1)]
-    for copy, (group, part) in zip(sent_c, order):
-        copy.wait_recv()
-        arrange(1 - c, group, part)
-    for copy in sent_x + sent_c:
+    arrange_own(1)
+    for k in range(2):
+        for copy, (group, part) in zip(sent_c[k], order[k]):
+            copy.wait_recv()
+            arrange(k, 1 - c, group, part)
+    for copy in sent_x[0] + sent_x[1] + sent_c[0] + sent_c[1]:
         copy.wait_send()
     wait_all(metas_x)
     meta = r.meta_x[0]
@@ -433,91 +465,129 @@
     ).astype(bf16)
 
     group_rows = NY * SLOTS
-    r.total[1, :, :, QUARTER:] = jnp.zeros((NX, group_rows, QUARTER), f32)
+    r.total[3] = jnp.zeros((NX, group_rows, QUARTER), f32)
     for q in range(4):
-        stop = quarter_stop(q)
-        half, low = q // 2, (q % 2) * QUARTER
-        r.total[half, :, :, low : low + stop - q * QUARTER] = lax.dot_general(
-            logit_grad, r.policy[:, q * QUARTER : stop], contract_first, preferred_element_type=f32
-        ).reshape(NX, group_rows, stop - q * QUARTER)
-    cores = []
-    for k, group in enumerate([far, right, left, x]):
-        r.outgoing[group] = r.total[1 - c, group].astype(bf16)
-        cores.append(send(r.outgoing.at[group], r.from_core.at[group], r.rc, k, across))
+        width = quarter_stop(q) - q * QUARTER
+        r.total[q, :, :, :width] = lax.dot_general(
+            logit_grad,
+            r.policy[:, q * QUARTER : quarter_stop(q)],
+            contract_first,
+            preferred_element_type=f32,
+        ).reshape(NX, group_rows, width)
     part_rows = PART * SLOTS
     low_part, high_part = slice(0, part_rows), slice(part_rows, 2 * part_rows)
-
-    def chip_sum(k, group):
-        cores[k].wait_recv()
-        return r.total[c, group] + r.from_core[group].astype(f32)
-
-    both = chip_sum(0, far)
-    r.send_x[far, 0] = both[low_part].astype(bf16)
-    r.send_x[far, 1] = both[high_part].astype(bf16)
-    reduced = [
-        send(r.send_x.at[far, 0], r.relay.at[0], r.rx, 0, to_right),
-        send(r.send_x.at[far, 1], r.relay.at[1], r.rx, 1, to_left),
-    ]
-    for_right = chip_sum(1, right)
-    r.send_x[right, 1] = for_right[high_part].astype(bf16)
-    reduced.append(send(r.send_x.at[right, 1], r.from_x.at[0], r.rx, 2, to_right))
-    r.total[c, right, low_part] = for_right[low_part]
-    for_left = chip_sum(2, left)
-    r.send_x[left, 0] = for_left[low_part].astype(bf16)
-    reduced.append(send(r.send_x.at[left, 0], r.from_x.at[1], r.rx, 3, to_left))
-    r.total[c, left, high_part] = for_left[high_part]
-    reduced[0].wait_recv()
-    r.send_x[right, 0] = (r.total[c, right, low_part] + r.relay[0].astype(f32)).astype(bf16)
-    reduced.append(send(r.send_x.at[right, 0], r.from_x.at[2], r.rx, 4, to_right))
-    reduced[1].wait_recv()
-    r.send_x[left, 1] = (r.total[c, left, high_part] + r.relay[1].astype(f32)).astype(bf16)
-    reduced.append(send(r.send_x.at[left, 1], r.from_x.at[3], r.rx, 5, to_left))
-    r.total[c, x] = chip_sum(3, x)
-    for copy in reduced[2:]:
-        copy.wait_recv()
-    pairs = [(low_part, 1, 2), (high_part, 0, 3)]
-    for part, (rows, first, second) in enumerate(pairs):
-        mine = r.total[c, x, rows] + r.from_x[first].astype(f32) + r.from_x[second].astype(f32)
-        mine = mine.reshape(PART, SLOTS, HALF)
-        packed = jnp.concatenate([mine[:, :, :QUARTER], mine[:, :, QUARTER:]], axis=1)
-        r.send_y[part * PART : (part + 1) * PART] = packed.astype(bf16)
-    copies = [
-        send(r.send_y.at[wrap(y + d, NY)], r.from_y.at[d], r.ry, d, along_y(d))
-        for d in range(1, NY)
-    ]
-    for copy in cores + reduced:
-        copy.wait_send()
-    wait_all(copies)
-    summed = r.send_y[y].astype(f32)
-    for k in range(1, NY):
-        summed += r.from_y[k].astype(f32)
-    r.from_z[z] = summed.astype(bf16)
-    wait_all([send(r.from_z.at[z], r.from_z.at[z], r.rz, d, along_z(d)) for d in range(1, NZ)])
-    summed = r.from_z[0].astype(f32)
-    for k in range(1, NZ):
-        summed += r.from_z[k].astype(f32)
-    r.final[c] = summed
-    copy = send(r.final.at[c], r.final.at[c], r.fc, 0, across)
-    load_proj.wait()
-    copy.wait()
-
-    slot_grad = 0.0
-    for q in range(4):
-        stop = quarter_stop(q)
-        part = r.final[q // 2, (q % 2) * SLOTS : (q % 2 + 1) * SLOTS, :][:, : stop - q * QUARTER]
-        r.hidden_grad[:, q * QUARTER : stop] = part
-        slot_grad += lax.dot_general(
-            r.proj[:, q * QUARTER : stop],
-            part.astype(bf16),
-            contract_last,
-            preferred_element_type=f32,
-        )
+    cores, reduced, copies_y, copies_z = [[], []], [[], []], [[], []], [[], []]
+    for k in range(2):
+        for i, group in enumerate([far, right, left, x]):
+            r.outgoing[k, group] = r.total[2 * (1 - c) + k, group].astype(bf16)
+            cores[k].append(
+                send(r.outgoing.at[k, group], r.from_core.at[k, group], r.rc, NX * k + i, across)
+            )
+
+    def pass_on(k, src, dst, target):
+        reduced[k].append(send(src, dst, r.rx, 6 * k + len(reduced[k]), target))
+
+    def chip_sum(k, i, group):
+        cores[k][i].wait_recv()
+        return r.total[2 * c + k, group] + r.from_core[k, group].astype(f32)
+
+    def start_far(k):
+        both = chip_sum(k, 0, far)
+        r.send_x[k, far, 0] = both[low_part].astype(bf16)
+        r.send_x[k, far, 1] = both[high_part].astype(bf16)
+        pass_on(k, r.send_x.at[k, far, 0], r.relay.at[k, 0], to_right)
+        pass_on(k, r.send_x.at[k, far, 1], r.relay.at[k, 1], to_left)
+
+    def start_direct(k):
+        for_right = chip_sum(k, 1, right)
+        r.send_x[k, right, 1] = for_right[high_part].astype(bf16)
+        pass_on(k, r.send_x.at[k, right, 1], r.from_x.at[k, 0], to_right)
+        r.total[2 * c + k, right, low_part] = for_right[low_part]
+        for_left = chip_sum(k, 2, left)
+        r.send_x[k, left, 0] = for_left[low_part].astype(bf16)
+        pass_on(k, r.send_x.at[k, left, 0], r.from_x.at[k, 1], to_left)
+        r.total[2 * c + k, left, high_part] = for_left[high_part]
+
+    def start_summed(k):
+        reduced[k][0].wait_recv()
+        block = r.total[2 * c + k, right, low_part] + r.relay[k, 0].astype(f32)
+        r.send_x[k, right, 0] = block.astype(bf16)
+        pass_on(k, r.send_x.at[k, right, 0], r.from_x.at[k, 2], to_right)
+        reduced[k][1].wait_recv()
+        block = r.total[2 * c + k, left, high_part] + r.relay[k, 1].astype(f32)
+        r.send_x[k, left, 1] = block.astype(bf16)
+        pass_on(k, r.send_x.at[k, left, 1], r.from_x.at[k, 3], to_left)
+        r.total[2 * c + k, x] = chip_sum(k, 3, x)
+
+    def start_y(k):
+        for copy in reduced[k][2:]:
+            copy.wait_recv()
+        for part, (rows, first, second) in enumerate([(low_part, 1, 2), (high_part, 0, 3)]):
+            mine = r.total[2 * c + k, x, rows] + r.from_x[k, first].astype(f32)
+            mine = (mine + r.from_x[k, second].astype(f32)).reshape(PART, SLOTS, QUARTER)
+            packed = jnp.concatenate([mine[:, :, :CHUNK], mine[:, :, CHUNK:]], axis=1)
+            r.send_y[k, part * PART : (part + 1) * PART] = packed.astype(bf16)
+        for d in far_first(NY):
+            copies_y[k].append(
+                send(
+                    r.send_y.at[k, wrap(y + d, NY)],
+                    r.from_y.at[k, d],
+                    r.ry,
+                    NY * k + d,
+                    along_y(d),
+                )
+            )
+
+    def start_z(k):
+        wait_all(copies_y[k])
+        summed = r.send_y[k, y].astype(f32)
+        for d in range(1, NY):
+            summed += r.from_y[k, d].astype(f32)
+        r.from_z[k, z] = summed.astype(bf16)
+        block = r.from_z.at[k, z]
+        for d in far_first(NZ):
+            copies_z[k].append(send(block, block, r.rz, NZ * k + d, along_z(d)))
+
+    def start_core(k):
+        wait_all(copies_z[k])
+        summed = r.from_z[k, 0].astype(f32)
+        for d in range(1, NZ):
+            summed += r.from_z[k, d].astype(f32)
+        r.final[2 * c + k] = summed
+        block = r.final.at[2 * c + k]
+        return send(block, block, r.fc, k, across)
+
+    start_far(0)
+    start_direct(0)
+    start_far(1)
+    start_summed(0)
+    start_direct(1)
+    start_summed(1)
+    start_y(0)
+    start_y(1)
+    start_z(0)
+    start_z(1)
     slot_row = lax.broadcasted_iota(jnp.int32, (SLOTS, tokens), 0)
     token = lax.broadcasted_iota(jnp.int32, (SLOTS, tokens), 1)
     landing = jnp.zeros((SLOTS, tokens), f32)
     for k in range(SLOTS):
         landing = jnp.where((slot_row == k) & (token == r.slot_pos[k]), 1.0, landing)
-    added = jnp.dot(slot_grad, landing, preferred_element_type=f32)
+    load_proj.wait()
+    finals = [start_core(0), start_core(1)]
+    slot_grad = 0.0
+    for k in range(2):
+        finals[k].wait()
+        for q in (k, 2 + k):
+            stop = quarter_stop(q)
+            part = jnp.concatenate([r.final[q, :SLOTS, :], r.final[q, SLOTS:, :]], axis=1)
+            part = part[:, : stop - q * QUARTER]
+            r.hidden_grad[:, q * QUARTER : stop] = part
+            slot_grad += jnp.dot(
+                part.astype(bf16), r.proj[q * QUARTER : stop, :], preferred_element_type=f32
+            )
+    for copy in cores[0] + cores[1] + reduced[0] + reduced[1]:
+        copy.wait_send()
+    added = lax.dot_general(slot_grad, landing, contract_first, preferred_element_type=f32)
     r.upper_t[...] = (r.upper_t[...] + added).astype(bf16).astype(f32)
 
     deltas = []
@@ -538,19 +608,13 @@
         grads = by_head(r.upper_t, t).astype(bf16)
         dprob = one_block(jnp.dot(r.value_ext[strip], grads, preferred_element_type=f32))
         dscore = both_blocks(r.prob[t] * (dprob - deltas[t]))
+        r.dscore[t] = dscore
         r.key_grad[:, strip] += lax.dot_general(
             by_head(r.query_t, t), dscore, contract_last, preferred_element_type=f32
         )
         r.value_grad[:, strip] += lax.dot_general(
             grads, r.prob_low[t], contract_last, preferred_element_type=f32
         )
-        query_grad = scale * lax.dot_general(
-            r.key_ext[strip], dscore, contract_first, preferred_element_type=f32
-        )
-        for h in range(heads):
-            r.query_grad[h * HD : (h + 1) * HD, t * WINDOW : (t + 1) * WINDOW] = query_grad[
-                :, h * WINDOW : (h + 1) * WINDOW
-            ]
     half_width = HD // 2
     mine_rows = pl.ds(pl.multiple_of(c * half_width, half_width), half_width)
     other_rows = pl.ds(pl.multiple_of((1 - c) * half_width, half_width), half_width)
@@ -570,6 +634,15 @@
         sink_sum += r.sink_y[k]
     r.sink_x[x] = sink_sum
     sinks_x = [send(r.sink_x.at[x], r.sink_x.at[x], r.kx, d, along_x(d)) for d in range(1, NX)]
+    for t in range(tiles):
+        strip = slice(t * WINDOW, (t + 2) * WINDOW)
+        query_grad = scale * lax.dot_general(
+            r.key_ext[strip], r.dscore[t], contract_first, preferred_element_type=f32
+        )
+        for h in range(heads):
+            r.query_grad[h * HD : (h + 1) * HD, t * WINDOW : (t + 1) * WINDOW] = query_grad[
+                :, h * WINDOW : (h + 1) * WINDOW
+            ]
     r.grad_queries[...] = jnp.transpose(r.query_grad[...]).astype(bf16)
     wait_all(kv_copies)
     for k, (grad, factor) in enumerate(both_grads):
@@ -582,7 +655,21 @@
     sink_sum = r.sink_x[0]
     for k in range(1, NX):
         sink_sum += r.sink_x[k]
-    r.grad_sinks[...] = jnp.broadcast_to(jnp.sum(sink_sum, axis=1, keepdims=True), (8, WINDOW))
+    for h in range(heads):
+        r.grad_sinks[h] = jnp.sum(sink_sum[h : h + 1])
+
+
+def hand_over(*refs):
+    count = (len(refs) - 1) // 2
+    sources, results, sems = refs[:count], refs[count : 2 * count], refs[-1]
+    copies = []
+    for k in range(count - 1):
+        copies.append(pltpu.make_async_copy(sources[k], results[k], sems.at[k]))
+        copies[k].start()
+    for h in range(results[-1].shape[0]):
+        results[-1][h] = sources[-1][h]
+    for copy in copies:
+        copy.wait()
 
 
 def shards(
@@ -608,39 +695,48 @@
     tokens = queries.shape[0]
     operands = [
         ("hidden", final_hidden, vmem),
-        ("advantages", advantages.astype(f32), smem),
+        ("advantages", advantages.reshape(1, SLOTS), vmem),
         ("sampled", sampled_ids, smem),
         ("live", slot_live, smem),
         ("slot_pos", slot_pos, smem),
         ("sinks", sinks, smem),
-        ("queries", queries, vmem),
-        ("upper", upper_grad, vmem),
+        ("queries_hbm", queries, hbm),
+        ("upper_hbm", upper_grad, hbm),
         ("docs", doc_ids.reshape(tokens // WINDOW, WINDOW), vmem),
         ("keys_hbm", keys, hbm),
         ("values_hbm", values, hbm),
-        ("proj_hbm", out_proj, hbm),
+        ("proj_hbm", out_proj.T, hbm),
         ("policy_hbm", policy_head, hbm),
         ("frozen_hbm", reference_head, hbm),
     ]
     results = [
-        ("grad_queries", jax.ShapeDtypeStruct(queries.shape, bf16)),
-        ("grad_kv", jax.ShapeDtypeStruct((2, HD // 2, tokens), bf16)),
-        ("grad_sinks", jax.ShapeDtypeStruct((8, WINDOW), f32)),
-        ("hidden_grad", jax.ShapeDtypeStruct(final_hidden.shape, f32)),
+        ("grad_queries", jax.ShapeDtypeStruct(queries.shape, bf16), vmem),
+        ("grad_kv", jax.ShapeDtypeStruct((2, HD // 2, tokens), bf16), vmem),
+        ("hidden_grad", jax.ShapeDtypeStruct(final_hidden.shape, f32), vmem),
+        ("grad_sinks", jax.ShapeDtypeStruct((heads,), f32), smem),
     ]
     scratch = named_scratch(heads, tokens, policy_head.shape[0])
-    names = [name for name, _, _ in operands] + [name for name, _ in results] + list(scratch)
-    grad_queries, grad_kv, grad_sinks, hidden_grad = pl.pallas_call(
+    names = [name for name, _, _ in operands + results] + list(scratch)
+    shapes = [shape for _, shape, _ in results]
+    made = pl.pallas_call(
         kernel_of(names),
-        out_shape=[shape for _, shape in results],
+        out_shape=shapes,
         in_specs=[spec for _, _, spec in operands],
-        out_specs=[vmem] * len(results),
+        out_specs=[spec for _, _, spec in results],
         scratch_shapes=list(scratch.values()),
         compiler_params=pltpu.CompilerParams(
             collective_id=0, has_side_effects=True, vmem_limit_bytes=56 * 2**20
         ),
     )(*[value for _, value, _ in operands])
-    return (grad_queries, grad_kv, grad_sinks[:heads, 0], hidden_grad)
+    grad_queries, grad_kv, hidden_grad, grad_sinks = pl.pallas_call(
+        hand_over,
+        out_shape=shapes,
+        in_specs=[hbm] * 3 + [smem],
+        out_specs=[hbm] * 3 + [smem],
+        scratch_shapes=[pltpu.SemaphoreType.DMA((3,))],
+        compiler_params=pltpu.CompilerParams(vmem_limit_bytes=60 * 2**20),
+    )(*made)
+    return (grad_queries, grad_kv, grad_sinks, hidden_grad)
 
 
 def solution(mesh):

time: 96.3 us -> 96.5 us (level)
  Pallas kernels: 85.6 us -> 95.6 us
  local copies, waits for them, and re-layouts: 8.54 us -> 0 us
  other arithmetic: 1.17 us -> 0 us
    pallas_call x1 -> x2, Pallas kernels: 85.6 us -> 95.6 us  [the longest x1 80.6 us: shards(): pl.pallas_call(kernel_of(names), out_shape=shapes, in_specs=[spec for _,...]
    unnamed x4 -> x0, local copies, waits for them, and re-layouts: 7.24 us -> none
    slice x1 -> x0, local copies, waits for them, and re-layouts: 1.3 us -> none  [shards(): return (grad_queries, grad_kv, grad_sinks[:heads, 0], hidden_grad)]
    convert_element_type x1 -> x0, other arithmetic: 1.17 us -> none  [shards(): advantages.astype(f32)]
where the time goes in v3:
time: 96.5 us; the launch traced here: 96.3 us
  Pallas kernels  95.6 us (99%)
    pallas_call x1, Pallas kernels, shards(): pl.pallas_call(kernel_of(names), out_shape=shapes, in_specs=[spec for _,...  80.6 us
    pallas_call x1, Pallas kernels, shards(): pl.pallas_call(hand_over, out_shape=shapes, in_specs=[hbm] * 3 + [smem],...  15.1 us

profile of v3, /device:TPU:1, one launch (start us, length us, event | category | flops | bytes accessed | tf_op | source)
XLA Modules:
  0.0 96.3 jit_solution(2396652889123307495)
XLA Ops:
  0.6 80.6 %shard_map.165 = (bf16[512,256]{1,0:T(8,128)(2,1)}, bf16[2,32,512]{2,1,0:T(8,128)(2,1)}, f32[8,2880]{1,0:T(8,128)}, f32[4]{0:T(128)}) custom-call(bf16[8,2880]{1,0:T(8,128)(2,1)} %refs_0_.1, bf16[1,8]{1,0:T(2,128)(2,1)} %bitcast.5, s32[8]{0:T(128)} %refs_2_.1, s32[8]{0:T(128)} %refs_3_.1, s32[8]{0:T(128)} %refs_4_.1, f32[4]{0:T(128)} %refs_5_.1, ...), custom_call_target="tpu_custom_call" | custom-call | tf_op jit(solution)/shard_map/pallas_call | solution.py:721
  81.2 15.1 %shard_map.166 = (bf16[512,256]{1,0:T(8,128)(2,1)}, bf16[2,32,512]{2,1,0:T(8,128)(2,1)}, f32[8,2880]{1,0:T(8,128)}, f32[4]{0:T(128)}) custom-call(bf16[512,256]{1,0:T(8,128)(2,1)} %get-tuple-element.12.refs_0_, bf16[2,32,512]{2,1,0:T(8,128)(2,1)} %get-tuple-element.13.refs_1_, f32[8,2880]{1,0:T(8,128)} %get-tuple-element.14.refs_2_, f32[4]{0:T(128)} %get-tuple-element.15.refs_3_), custom_call_target="tpu_custom_call" | custom-call | tf_op jit(solution)/shard_map/pallas_call | solution.py:731

commit v4 on v3

--- a/solution.py
+++ b/solution.py
@@ -121,7 +121,13 @@
         "final": pltpu.VMEM((4, 2 * SLOTS, CHUNK), f32),
         "queries": pltpu.VMEM((tokens, width), bf16),
         "upper": pltpu.VMEM((tokens, width), bf16),
-        "dscore": pltpu.VMEM((tiles, 2 * WINDOW, lanes), bf16),
+        "slot_hot": pltpu.VMEM((tokens, WINDOW), f32),
+        "slot_query": pltpu.VMEM((HD, WINDOW), bf16),
+        "slot_upper": pltpu.VMEM((HD, WINDOW), f32),
+        "slot_prob": pltpu.VMEM((tokens + WINDOW, WINDOW), f32),
+        "slot_attended": pltpu.VMEM((HD, WINDOW), f32),
+        "slot_share": pltpu.VMEM((1, WINDOW), f32),
+        "sink_bulk": pltpu.VMEM((8, WINDOW), f32),
         "load_sem": dma((7,)),
         "gy": dma((2, 2 * NY)),
         "gx": dma((2, 12)),
@@ -276,6 +282,7 @@
     key_row = lax.broadcasted_iota(jnp.int32, (WINDOW, WINDOW), 0)
     query_col = lax.broadcasted_iota(jnp.int32, (WINDOW, WINDOW), 1)
     earlier = key_row > query_col
+    query_row = lax.broadcasted_iota(jnp.int32, (1, WINDOW), 1)
 
     def per_head(block):
         return jnp.concatenate([block] * heads, axis=1)
@@ -320,15 +327,91 @@
         exp_terms = jnp.where(allowed, jnp.exp(masked - row_top), 0.0)
         sink_term = jnp.exp(sink_row - row_top)
         inverse = 1.0 / (jnp.sum(exp_terms, axis=0, keepdims=True) + sink_term)
-        prob = exp_terms * inverse
+        query_token = query_row + t * WINDOW
+        keep = jnp.ones((1, WINDOW), f32)
+        for k in range(SLOTS):
+            keep = jnp.where(query_token == r.slot_pos[k], 0.0, keep)
+        keep = per_head(keep)
+        prob = exp_terms * (inverse * keep)
         low = both_blocks(prob)
         r.prob[t] = prob
         r.prob_low[t] = low
-        r.share[t] = sink_term * inverse
+        r.share[t] = sink_term * inverse * keep
         r.attended[t] = lax.dot_general(
             r.value_ext[strip], low, contract_first, preferred_element_type=f32
         )
 
+    def attention_backward(t):
+        strip = slice(t * WINDOW, (t + 2) * WINDOW)
+        grads_wide = by_head(r.upper_t, t)
+        delta = jnp.sum(grads_wide * r.attended[t], axis=0, keepdims=True)
+        sink_part = r.share[t] * delta
+        for h in range(heads):
+            r.sink_bulk[h : h + 1] -= sink_part[:, h * WINDOW : (h + 1) * WINDOW]
+        grads = grads_wide.astype(bf16)
+        dprob = one_block(jnp.dot(r.value_ext[strip], grads, preferred_element_type=f32))
+        dscore = both_blocks(r.prob[t] * (dprob - delta))
+        r.key_grad[:, strip] += lax.dot_general(
+            by_head(r.query_t, t), dscore, contract_last, preferred_element_type=f32
+        )
+        r.value_grad[:, strip] += lax.dot_general(
+            grads, r.prob_low[t], contract_last, preferred_element_type=f32
+        )
+        query_grad = scale * lax.dot_general(
+            r.key_ext[strip], dscore, contract_first, preferred_element_type=f32
+        )
+        for h in range(heads):
+            r.query_grad[h * HD : (h + 1) * HD, t * WINDOW : (t + 1) * WINDOW] = query_grad[
+                :, h * WINDOW : (h + 1) * WINDOW
+            ]
+
+    lane_head = lax.div(query_row, SLOTS)
+
+    def head_hot(h):
+        return jnp.where(lane_head == h, r.slot_hot[...], 0.0).astype(bf16)
+
+    def slot_setup():
+        slot_of = lax.rem(query_row, SLOTS)
+        pos_row = jnp.full((1, WINDOW), -1, jnp.int32)
+        for k in range(SLOTS):
+            pos_row = jnp.where(slot_of == k, r.slot_pos[k], pos_row)
+        sink_slot = jnp.zeros((1, WINDOW), f32)
+        for h in range(heads):
+            sink_slot = jnp.where(lane_head == h, r.sinks[h], sink_slot)
+        used = lane_head < heads
+        token_row = lax.broadcasted_iota(jnp.int32, (tokens, WINDOW), 0)
+        r.slot_hot[...] = jnp.where((token_row == pos_row) & used, 1.0, 0.0)
+        doc_row = jnp.zeros((1, WINDOW), f32)
+        for t in range(tiles):
+            hot = r.slot_hot[t * WINDOW : (t + 1) * WINDOW]
+            doc_row += jnp.sum(hot * r.key_marks[t + 1], axis=0, keepdims=True)
+        query, upper = 0.0, 0.0
+        for h in range(heads):
+            hot, span = head_hot(h), slice(h * HD, (h + 1) * HD)
+            query += jnp.dot(r.query_t[span], hot, preferred_element_type=f32)
+            upper += jnp.dot(r.upper_t[span].astype(bf16), hot, preferred_element_type=f32)
+        r.slot_query[...] = query.astype(bf16)
+        r.slot_upper[...] = upper
+        scores = jnp.dot(r.key_ext[...], r.slot_query[...], preferred_element_type=f32)
+        key_at = lax.broadcasted_iota(jnp.int32, scores.shape, 0)
+        behind = pos_row + WINDOW - key_at
+        marks = r.key_marks[...].reshape(scores.shape)
+        allowed = (behind >= 0) & (behind < WINDOW) & (marks == doc_row) & used
+        masked = jnp.where(allowed, scores * scale, masked_score)
+        row_top = jnp.maximum(jnp.max(masked, axis=0, keepdims=True), sink_slot)
+        exp_terms = jnp.where(allowed, jnp.exp(masked - row_top), 0.0)
+        sink_term = jnp.exp(sink_slot - row_top)
+        inverse = 1.0 / (jnp.sum(exp_terms, axis=0, keepdims=True) + sink_term)
+        prob = exp_terms * inverse
+        r.slot_prob[...] = prob
+        r.slot_share[...] = jnp.where(used, sink_term * inverse, 0.0)
+        r.slot_attended[...] = lax.dot_general(
+            r.value_ext[...], prob.astype(bf16), contract_first, preferred_element_type=f32
+        )
+
+    r.key_grad[...] = jnp.zeros(r.key_grad.shape, f32)
+    r.value_grad[...] = jnp.zeros(r.value_grad.shape, f32)
+    r.sink_bulk[...] = jnp.zeros(r.sink_bulk.shape, f32)
     sent_x, sent_c, order = [[], []], [[], []], [[], []]
 
     def along(k, group, part, target):
@@ -441,16 +524,24 @@
     stats = [policy_peak + jnp.log(mass), frozen_peak + jnp.log(frozen_mass), mean]
 
     r.stat_xc[0] = fold(stats)
-    wait_all(
-        [
-            send(r.stat_xc.at[0], r.stat_xc.at[k + 1], r.sxc, k, along_x(d, o))
-            for k, (d, o) in enumerate(xc_steps)
-        ]
-    )
+    copies = [
+        send(r.stat_xc.at[0], r.stat_xc.at[k + 1], r.sxc, k, along_x(d, o))
+        for k, (d, o) in enumerate(xc_steps)
+    ]
+    attention_backward(0)
+    wait_all(copies)
     r.stat_y[0] = fold(merged([r.stat_xc[k] for k in range(NX * NC)]))
-    wait_all([send(r.stat_y.at[0], r.stat_y.at[d], r.sy, d, along_y(d)) for d in range(1, NY)])
+    copies = [
+        send(r.stat_y.at[0], r.stat_y.at[d], r.sy, d, along_y(d)) for d in far_first(NY)
+    ]
+    attention_backward(1)
+    wait_all(copies)
     r.stat_z[0] = fold(merged([r.stat_y[k] for k in range(NY)]))
-    wait_all([send(r.stat_z.at[0], r.stat_z.at[d], r.sz, d, along_z(d)) for d in range(1, NZ)])
+    copies = [
+        send(r.stat_z.at[0], r.stat_z.at[d], r.sz, d, along_z(d)) for d in far_first(NZ)
+    ]
+    attention_backward(2)
+    wait_all(copies)
     policy_lognorm, frozen_lognorm, cross_total = merged([r.stat_z[k] for k in range(NZ)])
 
     divergence = cross_total - policy_lognorm + frozen_lognorm
@@ -484,6 +575,9 @@
                 send(r.outgoing.at[k, group], r.from_core.at[k, group], r.rc, NX * k + i, across)
             )
 
+    for t in range(3, tiles):
+        attention_backward(t)
+
     def pass_on(k, src, dst, target):
         reduced[k].append(send(src, dst, r.rx, 6 * k + len(reduced[k]), target))
 
@@ -565,13 +659,9 @@
     start_summed(1)
     start_y(0)
     start_y(1)
+    slot_setup()
     start_z(0)
     start_z(1)
-    slot_row = lax.broadcasted_iota(jnp.int32, (SLOTS, tokens), 0)
-    token = lax.broadcasted_iota(jnp.int32, (SLOTS, tokens), 1)
-    landing = jnp.zeros((SLOTS, tokens), f32)
-    for k in range(SLOTS):
-        landing = jnp.where((slot_row == k) & (token == r.slot_pos[k]), 1.0, landing)
     load_proj.wait()
     finals = [start_core(0), start_core(1)]
     slot_grad = 0.0
@@ -587,34 +677,34 @@
             )
     for copy in cores[0] + cores[1] + reduced[0] + reduced[1]:
         copy.wait_send()
-    added = lax.dot_general(slot_grad, landing, contract_first, preferred_element_type=f32)
-    r.upper_t[...] = (r.upper_t[...] + added).astype(bf16).astype(f32)
-
-    deltas = []
-    sink_total = 0.0
-    for t in range(tiles):
-        delta = jnp.sum(by_head(r.upper_t, t) * r.attended[t], axis=0, keepdims=True)
-        deltas.append(delta)
-        sink_total += r.share[t] * delta
-    sink_rows = [-sink_total[:, h * WINDOW : (h + 1) * WINDOW] for h in range(heads)]
-    sink_rows.append(jnp.zeros((8 - heads, WINDOW), f32))
-    r.sink_y[y] = jnp.concatenate(sink_rows, axis=0)
-    sinks_y = [send(r.sink_y.at[y], r.sink_y.at[y], r.ky, d, along_y(d)) for d in range(1, NY)]
-
-    r.key_grad[...] = jnp.zeros(r.key_grad.shape, f32)
-    r.value_grad[...] = jnp.zeros(r.value_grad.shape, f32)
-    for t in range(tiles):
-        strip = slice(t * WINDOW, (t + 2) * WINDOW)
-        grads = by_head(r.upper_t, t).astype(bf16)
-        dprob = one_block(jnp.dot(r.value_ext[strip], grads, preferred_element_type=f32))
-        dscore = both_blocks(r.prob[t] * (dprob - deltas[t]))
-        r.dscore[t] = dscore
-        r.key_grad[:, strip] += lax.dot_general(
-            by_head(r.query_t, t), dscore, contract_last, preferred_element_type=f32
-        )
-        r.value_grad[:, strip] += lax.dot_general(
-            grads, r.prob_low[t], contract_last, preferred_element_type=f32
-        )
+    slot_at = lax.broadcasted_iota(jnp.int32, (SLOTS, WINDOW), 0)
+    spread_out = lax.rem(lax.broadcasted_iota(jnp.int32, (SLOTS, WINDOW), 1), SLOTS) == slot_at
+    wide_grad = lax.dot_general(
+        slot_grad,
+        spread_out.astype(f32),
+        contract_first,
+        precision=lax.Precision.HIGHEST,
+        preferred_element_type=f32,
+    )
+    slot_out = r.slot_upper[...]
+    for h in range(heads):
+        slot_out += jnp.where(lane_head == h, wide_grad[h * HD : (h + 1) * HD], 0.0)
+    slot_low = slot_out.astype(bf16)
+    slot_delta = jnp.sum(slot_low.astype(f32) * r.slot_attended[...], axis=0, keepdims=True)
+    slot_sink = r.slot_share[...] * slot_delta
+    sink_heads = lax.broadcasted_iota(jnp.int32, (8, WINDOW), 0) == lane_head
+    r.sink_y[y] = r.sink_bulk[...] - jnp.where(sink_heads, slot_sink, 0.0)
+    sinks_y = [
+        send(r.sink_y.at[y], r.sink_y.at[y], r.ky, d, along_y(d)) for d in far_first(NY)
+    ]
+    slot_dprob = jnp.dot(r.value_ext[...], slot_low, preferred_element_type=f32)
+    slot_dscore = (r.slot_prob[...] * (slot_dprob - slot_delta)).astype(bf16)
+    r.key_grad[...] += lax.dot_general(
+        r.slot_query[...], slot_dscore, contract_last, preferred_element_type=f32
+    )
+    r.value_grad[...] += lax.dot_general(
+        slot_low, r.slot_prob[...].astype(bf16), contract_last, preferred_element_type=f32
+    )
     half_width = HD // 2
     mine_rows = pl.ds(pl.multiple_of(c * half_width, half_width), half_width)
     other_rows = pl.ds(pl.multiple_of((1 - c) * half_width, half_width), half_width)
@@ -628,21 +718,20 @@
         send(r.edge_send.at[1], r.edge_recv.at[1], r.kv, 1, (prev, z * NC + 1 - c)),
         send(r.kv_send, r.kv_recv, r.kv, 2, across),
     ]
+    slot_query_grad = scale * lax.dot_general(
+        r.key_ext[...], slot_dscore, contract_first, preferred_element_type=f32
+    )
+    slot_query_low = slot_query_grad.astype(bf16)
+    for h in range(heads):
+        r.query_grad[h * HD : (h + 1) * HD] += lax.dot_general(
+            slot_query_low, head_hot(h), contract_last, preferred_element_type=f32
+        )
     wait_all(sinks_y)
     sink_sum = r.sink_y[0]
     for k in range(1, NY):
         sink_sum += r.sink_y[k]
     r.sink_x[x] = sink_sum
     sinks_x = [send(r.sink_x.at[x], r.sink_x.at[x], r.kx, d, along_x(d)) for d in range(1, NX)]
-    for t in range(tiles):
-        strip = slice(t * WINDOW, (t + 2) * WINDOW)
-        query_grad = scale * lax.dot_general(
-            r.key_ext[strip], r.dscore[t], contract_first, preferred_element_type=f32
-        )
-        for h in range(heads):
-            r.query_grad[h * HD : (h + 1) * HD, t * WINDOW : (t + 1) * WINDOW] = query_grad[
-                :, h * WINDOW : (h + 1) * WINDOW
-            ]
     r.grad_queries[...] = jnp.transpose(r.query_grad[...]).astype(bf16)
     wait_all(kv_copies)
     for k, (grad, factor) in enumerate(both_grads):
@@ -660,16 +749,11 @@
 
 
 def hand_over(*refs):
-    count = (len(refs) - 1) // 2
-    sources, results, sems = refs[:count], refs[count : 2 * count], refs[-1]
-    copies = []
-    for k in range(count - 1):
-        copies.append(pltpu.make_async_copy(sources[k], results[k], sems.at[k]))
-        copies[k].start()
-    for h in range(results[-1].shape[0]):
-        results[-1][h] = sources[-1][h]
-    for copy in copies:
-        copy.wait()
+    count = len(refs) // 2
+    for source, result in zip(refs[: count - 1], refs[count:]):
+        result[...] = source[...]
+    for h in range(refs[-1].shape[0]):
+        refs[-1][h] = refs[count - 1][h]
 
 
 def shards(
@@ -731,9 +815,8 @@
     grad_queries, grad_kv, hidden_grad, grad_sinks = pl.pallas_call(
         hand_over,
         out_shape=shapes,
-        in_specs=[hbm] * 3 + [smem],
-        out_specs=[hbm] * 3 + [smem],
-        scratch_shapes=[pltpu.SemaphoreType.DMA((3,))],
+        in_specs=[spec for _, _, spec in results],
+        out_specs=[spec for _, _, spec in results],
         compiler_params=pltpu.CompilerParams(vmem_limit_bytes=60 * 2**20),
     )(*made)
     return (grad_queries, grad_kv, grad_sinks, hidden_grad)

time: 96.5 us -> 83.2 us (0.86)
  Pallas kernels: 95.6 us -> 82.4 us
    pallas_call x1, Pallas kernels: 15.1 us -> 1.78 us  [shards(): pl.pallas_call(hand_over, out_shape=shapes, in_specs=[spec for _, _, spec...]
where the time goes in v4:
time: 83.2 us; the launch traced here: 83 us
  Pallas kernels  82.4 us (99%)
    pallas_call x1, Pallas kernels, shards(): pl.pallas_call(kernel_of(names), out_shape=shapes, in_specs=[spec for _,...  80.6 us
    pallas_call x1, Pallas kernels, shards(): pl.pallas_call(hand_over, out_shape=shapes, in_specs=[spec for _, _, spec...  1.78 us

profile of v4, /device:TPU:1, one launch (start us, length us, event | category | flops | bytes accessed | tf_op | source)
XLA Modules:
  0.0 83.0 jit_solution(16182614473973634847)
XLA Ops:
  0.6 80.6 %shard_map.165 = (bf16[512,256]{1,0:T(8,128)(2,1)}, bf16[2,32,512]{2,1,0:T(8,128)(2,1)}, f32[8,2880]{1,0:T(8,128)}, f32[4]{0:T(128)}) custom-call(bf16[8,2880]{1,0:T(8,128)(2,1)} %refs_0_.1, bf16[1,8]{1,0:T(2,128)(2,1)} %bitcast.5, s32[8]{0:T(128)} %refs_2_.1, s32[8]{0:T(128)} %refs_3_.1, s32[8]{0:T(128)} %refs_4_.1, f32[4]{0:T(128)} %refs_5_.1, ...), custom_call_target="tpu_custom_call" | custom-call | tf_op jit(solution)/shard_map/pallas_call | solution.py:805
  81.3 1.8 %shard_map.166 = (bf16[512,256]{1,0:T(8,128)(2,1)}, bf16[2,32,512]{2,1,0:T(8,128)(2,1)}, f32[8,2880]{1,0:T(8,128)}, f32[4]{0:T(128)}) custom-call(bf16[512,256]{1,0:T(8,128)(2,1)} %get-tuple-element.12.refs_0_, bf16[2,32,512]{2,1,0:T(8,128)(2,1)} %get-tuple-element.13.refs_1_, f32[8,2880]{1,0:T(8,128)} %get-tuple-element.14.refs_2_, f32[4]{0:T(128)} %get-tuple-element.15.refs_3_), custom_call_target="tpu_custom_call" | custom-call | tf_op jit(solution)/shard_map/pallas_call | solution.py:815

commit v5 on v4

--- a/solution.py
+++ b/solution.py
@@ -99,8 +99,8 @@
         "kv_recv": pltpu.VMEM((2, HD // 2, tokens), bf16),
         "edge_send": pltpu.VMEM((2, 2, HD // 2, WINDOW), bf16),
         "edge_recv": pltpu.VMEM((2, 2, HD // 2, WINDOW), bf16),
-        "sink_y": pltpu.VMEM((NY, 8, WINDOW), f32),
-        "sink_x": pltpu.VMEM((NX, 8, WINDOW), f32),
+        "sink_y": pltpu.VMEM((NY, 1, WINDOW), f32),
+        "sink_x": pltpu.VMEM((NX, 1, WINDOW), f32),
         "wide": pltpu.VMEM((4, SLOTS, QUARTER), f32),
         "gathered": pltpu.VMEM((2, 2, NX, 2, PART, 2 * SLOTS, CHUNK), bf16),
         "rows": pltpu.VMEM((4, rows, QUARTER), bf16),
@@ -128,7 +128,19 @@
         "slot_attended": pltpu.VMEM((HD, WINDOW), f32),
         "slot_share": pltpu.VMEM((1, WINDOW), f32),
         "sink_bulk": pltpu.VMEM((8, WINDOW), f32),
-        "load_sem": dma((7,)),
+        "hidden": pltpu.VMEM((SLOTS, D), bf16),
+        "advantages": pltpu.VMEM((1, SLOTS), bf16),
+        "docs": pltpu.VMEM((tiles, WINDOW), jnp.int32),
+        "sampled": pltpu.SMEM((SLOTS,), jnp.int32),
+        "live": pltpu.SMEM((SLOTS,), jnp.int32),
+        "slot_pos": pltpu.SMEM((SLOTS,), jnp.int32),
+        "sinks": pltpu.SMEM((heads,), f32),
+        "grad_queries": pltpu.VMEM((tokens, width), bf16),
+        "grad_kv": pltpu.VMEM((2, HD // 2, tokens), bf16),
+        "hidden_grad": pltpu.VMEM((SLOTS, D), f32),
+        "logits": pltpu.VMEM((2, vocab_rows, rows), f32),
+        "load_sem": dma((14,)),
+        "store_sem": dma((3,)),
         "gy": dma((2, 2 * NY)),
         "gx": dma((2, 12)),
         "gc": dma((2, 16)),
@@ -175,20 +187,6 @@
     left, right, far = wrap(x - 1, NX), wrap(x + 1, NX), wrap(x + 2, NX)
     y_part, y_sub = lax.div(y, PART), lax.rem(y, PART)
 
-    def load(src, dst, k):
-        copy = pltpu.make_async_copy(src, dst, r.load_sem.at[k])
-        copy.start()
-        return copy
-
-    column = pl.multiple_of(lax.div(z, 2) * 128, 128)
-    load_keys = load(r.keys_hbm.at[:, pl.ds(column, 128)], r.key_cols, 0)
-    load_values = load(r.values_hbm.at[:, pl.ds(column, 128)], r.value_cols, 1)
-    load_policy = load(r.policy_hbm, r.policy, 2)
-    load_frozen = load(r.frozen_hbm, r.frozen, 3)
-    load_proj = load(r.proj_hbm, r.proj, 4)
-    load_queries = load(r.queries_hbm, r.queries, 5)
-    load_upper = load(r.upper_hbm, r.upper, 6)
-
     def along_x(d, other=0):
         return device(wrap(x + d, NX), y, z, 1 - c if other else c)
 
@@ -226,6 +224,30 @@
     for peer in peers:
         pl.semaphore_signal(barrier, inc=1, device_id=peer, device_id_type=MESH)
 
+    def load(src, dst, k):
+        copy = pltpu.make_async_copy(src, dst, r.load_sem.at[k])
+        copy.start()
+        return copy
+
+    load_hidden = load(r.hidden_hbm, r.hidden, 0)
+    small = [
+        load(r.advantages_hbm, r.advantages, 1),
+        load(r.sampled_hbm, r.sampled, 2),
+        load(r.live_hbm, r.live, 3),
+        load(r.slot_pos_hbm, r.slot_pos, 4),
+        load(r.sinks_hbm, r.sinks, 5),
+        load(r.docs_hbm, r.docs, 6),
+    ]
+    column = pl.multiple_of(lax.div(z, 2) * 128, 128)
+    load_keys = load(r.keys_hbm.at[:, pl.ds(column, 128)], r.key_cols, 7)
+    load_values = load(r.values_hbm.at[:, pl.ds(column, 128)], r.value_cols, 8)
+    load_queries = load(r.queries_hbm, r.queries, 9)
+    load_upper = load(r.upper_hbm, r.upper, 10)
+    load_policy = load(r.policy_hbm, r.policy, 11)
+    load_frozen = load(r.frozen_hbm, r.frozen, 12)
+    load_proj = load(r.proj_hbm, r.proj, 13)
+
+    load_hidden.wait()
     hidden = r.hidden[...].astype(f32)
     r.wide[3] = jnp.zeros((SLOTS, QUARTER), f32)
     for q in range(4):
@@ -233,6 +255,7 @@
     packed = jnp.concatenate([r.wide[2 * c], r.wide[2 * c + 1]], axis=0).astype(bf16)
     for k in range(2):
         r.gathered[k, c, x, y_part, y_sub] = packed[:, k * CHUNK : (k + 1) * CHUNK]
+    wait_all(small)
     stat = r.meta_y.shape[1:]
     field = lax.broadcasted_iota(jnp.int32, stat, 0)
     lane = lax.broadcasted_iota(jnp.int32, stat, 1) + jnp.where(field < 3, 0, stat[1])
@@ -486,10 +509,30 @@
     for t in range(3, tiles):
         attention_forward(t)
     arrange_own(1)
+    load_policy.wait()
+    load_frozen.wait()
+
+    def add_logits(half, first):
+        for i, head in enumerate([r.policy, r.frozen]):
+            result = 0.0
+            for q in (2 * half, 2 * half + 1):
+                width = quarter_stop(q) - q * QUARTER
+                result += lax.dot_general(
+                    head[:, q * QUARTER : quarter_stop(q)],
+                    r.rows[q, :, :width],
+                    contract_last,
+                    preferred_element_type=f32,
+                )
+            r.logits[i] = result if first else r.logits[i] + result
+
+    for half in range(2):
+        pl.when(c == half)(lambda half=half: add_logits(half, True))
     for k in range(2):
         for copy, (group, part) in zip(sent_c[k], order[k]):
             copy.wait_recv()
             arrange(k, 1 - c, group, part)
+    for half in range(2):
+        pl.when(c != half)(lambda half=half: add_logits(half, False))
     for copy in sent_x[0] + sent_x[1] + sent_c[0] + sent_c[1]:
         copy.wait_send()
     wait_all(metas_x)
@@ -497,23 +540,7 @@
     for k in range(1, NX):
         meta += r.meta_x[k]
 
-    load_policy.wait()
-    load_frozen.wait()
-
-    def logits_of(head):
-        result = 0.0
-        for q in range(4):
-            stop = quarter_stop(q)
-            result += lax.dot_general(
-                head[:, q * QUARTER : stop],
-                r.rows[q, :, : stop - q * QUARTER],
-                contract_last,
-                preferred_element_type=f32,
-            )
-        return result
-
-    policy_logits = logits_of(r.policy)
-    frozen_logits = logits_of(r.frozen)
+    policy_logits, frozen_logits = r.logits[0], r.logits[1]
     policy_peak = jnp.max(policy_logits, axis=0, keepdims=True)
     frozen_peak = jnp.max(frozen_logits, axis=0, keepdims=True)
     logit_diff = policy_logits - frozen_logits
@@ -556,15 +583,25 @@
     ).astype(bf16)
 
     group_rows = NY * SLOTS
-    r.total[3] = jnp.zeros((NX, group_rows, QUARTER), f32)
-    for q in range(4):
-        width = quarter_stop(q) - q * QUARTER
-        r.total[q, :, :, :width] = lax.dot_general(
+    r.total[3, :, :, D - 3 * QUARTER - 64 :] = jnp.zeros(
+        (NX, group_rows, 4 * QUARTER - D + 64), f32
+    )
+
+    def product(half):
+        stop = quarter_stop(2 * half + 1)
+        whole = lax.dot_general(
             logit_grad,
-            r.policy[:, q * QUARTER : quarter_stop(q)],
+            r.policy[:, half * HALF : stop],
             contract_first,
             preferred_element_type=f32,
-        ).reshape(NX, group_rows, width)
+        )
+        for q in (2 * half, 2 * half + 1):
+            width = quarter_stop(q) - q * QUARTER
+            low = (q - 2 * half) * QUARTER
+            r.total[q, :, :, :width] = whole[:, low : low + width].reshape(NX, group_rows, width)
+
+    for half in range(2):
+        pl.when(c != half)(lambda half=half: product(half))
     part_rows = PART * SLOTS
     low_part, high_part = slice(0, part_rows), slice(part_rows, 2 * part_rows)
     cores, reduced, copies_y, copies_z = [[], []], [[], []], [[], []], [[], []]
@@ -575,6 +612,8 @@
                 send(r.outgoing.at[k, group], r.from_core.at[k, group], r.rc, NX * k + i, across)
             )
 
+    for half in range(2):
+        pl.when(c == half)(lambda half=half: product(half))
     for t in range(3, tiles):
         attention_backward(t)
 
@@ -677,6 +716,14 @@
             )
     for copy in cores[0] + cores[1] + reduced[0] + reduced[1]:
         copy.wait_send()
+    stores = []
+
+    def store(src, dst):
+        copy = pltpu.make_async_copy(src, dst, r.store_sem.at[len(stores)])
+        copy.start()
+        stores.append(copy)
+
+    store(r.hidden_grad, r.hidden_grad_hbm)
     slot_at = lax.broadcasted_iota(jnp.int32, (SLOTS, WINDOW), 0)
     spread_out = lax.rem(lax.broadcasted_iota(jnp.int32, (SLOTS, WINDOW), 1), SLOTS) == slot_at
     wide_grad = lax.dot_general(
@@ -692,8 +739,10 @@
     slot_low = slot_out.astype(bf16)
     slot_delta = jnp.sum(slot_low.astype(f32) * r.slot_attended[...], axis=0, keepdims=True)
     slot_sink = r.slot_share[...] * slot_delta
-    sink_heads = lax.broadcasted_iota(jnp.int32, (8, WINDOW), 0) == lane_head
-    r.sink_y[y] = r.sink_bulk[...] - jnp.where(sink_heads, slot_sink, 0.0)
+    sink_heads = lax.broadcasted_iota(jnp.int32, (8, WINDOW), 0)
+    sink_block = r.sink_bulk[...] - jnp.where(sink_heads == lane_head, slot_sink, 0.0)
+    sink_sums = jnp.sum(sink_block, axis=1, keepdims=True)
+    r.sink_y[y] = jnp.sum(jnp.where(sink_heads == query_row, sink_sums, 0.0), axis=0, keepdims=True)
     sinks_y = [
         send(r.sink_y.at[y], r.sink_y.at[y], r.ky, d, along_y(d)) for d in far_first(NY)
     ]
@@ -733,6 +782,7 @@
     r.sink_x[x] = sink_sum
     sinks_x = [send(r.sink_x.at[x], r.sink_x.at[x], r.kx, d, along_x(d)) for d in range(1, NX)]
     r.grad_queries[...] = jnp.transpose(r.query_grad[...]).astype(bf16)
+    store(r.grad_queries, r.grad_queries_hbm)
     wait_all(kv_copies)
     for k, (grad, factor) in enumerate(both_grads):
         own = grad[mine_rows, WINDOW:] * factor + r.kv_recv[k].astype(f32)
@@ -740,12 +790,14 @@
         r.grad_kv[k] = jnp.concatenate(
             [own[:, : tokens - WINDOW], own[:, tokens - WINDOW :] + edge], axis=1
         ).astype(bf16)
+    store(r.grad_kv, r.grad_kv_hbm)
     wait_all(sinks_x)
     sink_sum = r.sink_x[0]
     for k in range(1, NX):
         sink_sum += r.sink_x[k]
     for h in range(heads):
-        r.grad_sinks[h] = jnp.sum(sink_sum[h : h + 1])
+        r.grad_sinks[h] = jnp.sum(jnp.where(query_row == h, sink_sum, 0.0))
+    wait_all(stores)
 
 
 def hand_over(*refs):
@@ -778,40 +830,40 @@
     heads = sinks.shape[0]
     tokens = queries.shape[0]
     operands = [
-        ("hidden", final_hidden, vmem),
-        ("advantages", advantages.reshape(1, SLOTS), vmem),
-        ("sampled", sampled_ids, smem),
-        ("live", slot_live, smem),
-        ("slot_pos", slot_pos, smem),
-        ("sinks", sinks, smem),
-        ("queries_hbm", queries, hbm),
-        ("upper_hbm", upper_grad, hbm),
-        ("docs", doc_ids.reshape(tokens // WINDOW, WINDOW), vmem),
-        ("keys_hbm", keys, hbm),
-        ("values_hbm", values, hbm),
-        ("proj_hbm", out_proj.T, hbm),
-        ("policy_hbm", policy_head, hbm),
-        ("frozen_hbm", reference_head, hbm),
+        ("hidden_hbm", final_hidden),
+        ("advantages_hbm", advantages.reshape(1, SLOTS)),
+        ("sampled_hbm", sampled_ids),
+        ("live_hbm", slot_live),
+        ("slot_pos_hbm", slot_pos),
+        ("sinks_hbm", sinks),
+        ("docs_hbm", doc_ids.reshape(tokens // WINDOW, WINDOW)),
+        ("queries_hbm", queries),
+        ("upper_hbm", upper_grad),
+        ("keys_hbm", keys),
+        ("values_hbm", values),
+        ("proj_hbm", out_proj.T),
+        ("policy_hbm", policy_head),
+        ("frozen_hbm", reference_head),
     ]
     results = [
-        ("grad_queries", jax.ShapeDtypeStruct(queries.shape, bf16), vmem),
-        ("grad_kv", jax.ShapeDtypeStruct((2, HD // 2, tokens), bf16), vmem),
-        ("hidden_grad", jax.ShapeDtypeStruct(final_hidden.shape, f32), vmem),
+        ("grad_queries_hbm", jax.ShapeDtypeStruct(queries.shape, bf16), vmem),
+        ("grad_kv_hbm", jax.ShapeDtypeStruct((2, HD // 2, tokens), bf16), vmem),
+        ("hidden_grad_hbm", jax.ShapeDtypeStruct(final_hidden.shape, f32), vmem),
         ("grad_sinks", jax.ShapeDtypeStruct((heads,), f32), smem),
     ]
     scratch = named_scratch(heads, tokens, policy_head.shape[0])
-    names = [name for name, _, _ in operands + results] + list(scratch)
+    names = [entry[0] for entry in operands + results] + list(scratch)
     shapes = [shape for _, shape, _ in results]
     made = pl.pallas_call(
         kernel_of(names),
         out_shape=shapes,
-        in_specs=[spec for _, _, spec in operands],
-        out_specs=[spec for _, _, spec in results],
+        in_specs=[hbm] * len(operands),
+        out_specs=[hbm] * 3 + [smem],
         scratch_shapes=list(scratch.values()),
         compiler_params=pltpu.CompilerParams(
             collective_id=0, has_side_effects=True, vmem_limit_bytes=56 * 2**20
         ),
-    )(*[value for _, value, _ in operands])
+    )(*[value for _, value in operands])
     grad_queries, grad_kv, hidden_grad, grad_sinks = pl.pallas_call(
         hand_over,
         out_shape=shapes,

time: 83.2 us -> 82.1 us (0.987)
  Pallas kernels: 82.4 us -> 81.3 us
    pallas_call x1, Pallas kernels: 80.6 us -> 79.5 us  [shards(): pl.pallas_call(kernel_of(names), out_shape=shapes, in_specs=[hbm] * len(o...]
where the time goes in v5:
time: 82.1 us; the launch traced here: 81.9 us
  Pallas kernels  81.3 us (99%)
    pallas_call x1, Pallas kernels, shards(): pl.pallas_call(kernel_of(names), out_shape=shapes, in_specs=[hbm] * len(o...  79.5 us
    pallas_call x1, Pallas kernels, shards(): pl.pallas_call(hand_over, out_shape=shapes, in_specs=[spec for _, _, spec...  1.78 us

profile of v5, /device:TPU:1, one launch (start us, length us, event | category | flops | bytes accessed | tf_op | source)
XLA Modules:
  0.0 81.9 jit_solution(13974051210292948906)
XLA Ops:
  0.6 79.5 %shard_map.165 = (bf16[512,256]{1,0:T(8,128)(2,1)}, bf16[2,32,512]{2,1,0:T(8,128)(2,1)}, f32[8,2880]{1,0:T(8,128)}, f32[4]{0:T(128)}) custom-call(bf16[8,2880]{1,0:T(8,128)(2,1)} %refs_0_.1, bf16[1,8]{1,0:T(2,128)(2,1)} %bitcast.5, s32[8]{0:T(128)} %refs_2_.1, s32[8]{0:T(128)} %refs_3_.1, s32[8]{0:T(128)} %refs_4_.1, f32[4]{0:T(128)} %refs_5_.1, ...), custom_call_target="tpu_custom_call" | custom-call | tf_op jit(solution)/shard_map/pallas_call | solution.py:857
  80.2 1.8 %shard_map.166 = (bf16[512,256]{1,0:T(8,128)(2,1)}, bf16[2,32,512]{2,1,0:T(8,128)(2,1)}, f32[8,2880]{1,0:T(8,128)}, f32[4]{0:T(128)}) custom-call(bf16[512,256]{1,0:T(8,128)(2,1)} %get-tuple-element.12.refs_0_, bf16[2,32,512]{2,1,0:T(8,128)(2,1)} %get-tuple-element.13.refs_1_, f32[8,2880]{1,0:T(8,128)} %get-tuple-element.14.refs_2_, f32[4]{0:T(128)} %get-tuple-element.15.refs_3_), custom_call_target="tpu_custom_call" | custom-call | tf_op jit(solution)/shard_map/pallas_call | solution.py:867

commit v6 on v5

--- a/solution.py
+++ b/solution.py
@@ -14,6 +14,7 @@
 SLOTS = 8
 PART = NY // 2
 CHUNK = QUARTER // 2
+TILES = CHUNK // 128
 
 loss_scale = 64.0
 kl_weight = 1.0
@@ -44,18 +45,18 @@
 
 
 def merged(blocks):
-    rows = [[unfold(block, k) for block in blocks] for k in range(3)]
-    tops = [rows[0][0], rows[1][0]]
-    for k in range(2):
-        for row in rows[k][1:]:
-            tops[k] = jnp.maximum(tops[k], row)
-    mass, cross, frozen = 0.0, 0.0, 0.0
-    for policy, other, mean in zip(*rows):
-        share = jnp.exp(policy - tops[0])
+    top = blocks[0]
+    for block in blocks[1:]:
+        top = jnp.maximum(top, block)
+    mass, cross = 0.0, 0.0
+    for block in blocks:
+        share = jnp.exp(block - top)
         mass += share
-        cross += share * mean
-        frozen += jnp.exp(other - tops[1])
-    return [tops[0] + jnp.log(mass), tops[1] + jnp.log(frozen), cross / mass]
+        cross += pltpu.roll(share, 2, axis=0) * block
+    row = lax.broadcasted_iota(jnp.int32, top.shape, 0)
+    return jnp.where(
+        (row == 2) | (row == 5), cross / pltpu.roll(mass, 2, axis=0), top + jnp.log(mass)
+    )
 
 
 def far_first(size):
@@ -117,8 +118,9 @@
         "from_x": pltpu.VMEM((2, 4, PART * SLOTS, QUARTER), bf16),
         "send_y": pltpu.VMEM((2, NY, 2 * SLOTS, CHUNK), bf16),
         "from_y": pltpu.VMEM((2, NY, 2 * SLOTS, CHUNK), bf16),
-        "from_z": pltpu.VMEM((2, NZ, 2 * SLOTS, CHUNK), bf16),
-        "final": pltpu.VMEM((4, 2 * SLOTS, CHUNK), f32),
+        "send_z": pltpu.VMEM((2 * TILES, 2 * SLOTS, 128), bf16),
+        "from_z": pltpu.VMEM((NZ, 2 * SLOTS, 128), bf16),
+        "final": pltpu.VMEM((NC, 2 * TILES, 2 * SLOTS, 128), bf16),
         "queries": pltpu.VMEM((tokens, width), bf16),
         "upper": pltpu.VMEM((tokens, width), bf16),
         "slot_hot": pltpu.VMEM((tokens, WINDOW), f32),
@@ -152,8 +154,8 @@
         "rc": dma((2, 2 * NX)),
         "rx": dma((2, 12)),
         "ry": dma((2, 2 * NY)),
-        "rz": dma((2, 2 * NZ)),
-        "fc": dma((2, 2)),
+        "rz": dma((2, NZ)),
+        "fc": dma((2, NC * NZ)),
         "halo": dma((2, 2)),
         "kv": dma((2, 3)),
         "ky": dma((2, NY)),
@@ -218,8 +220,8 @@
             copy.wait()
 
     barrier = pltpu.get_barrier_semaphore()
-    peers = [along_x(d, o) for d, o in xc_steps]
-    peers += [along_y(d) for d in range(1, NY)] + [along_z(d) for d in range(1, NZ)]
+    peers = [along_y(d) for d in far_first(NY)] + [along_x(d, o) for d, o in xc_steps]
+    peers += [device(x, y, wrap(z + d, NZ), o) for d in far_first(NZ) for o in range(NC)]
     peers += [(owner, z * NC + o) for owner in (prev, after) for o in range(NC)]
     for peer in peers:
         pl.semaphore_signal(barrier, inc=1, device_id=peer, device_id_type=MESH)
@@ -557,19 +559,20 @@
     ]
     attention_backward(0)
     wait_all(copies)
-    r.stat_y[0] = fold(merged([r.stat_xc[k] for k in range(NX * NC)]))
+    r.stat_y[0] = merged([r.stat_xc[k] for k in range(NX * NC)])
     copies = [
         send(r.stat_y.at[0], r.stat_y.at[d], r.sy, d, along_y(d)) for d in far_first(NY)
     ]
     attention_backward(1)
     wait_all(copies)
-    r.stat_z[0] = fold(merged([r.stat_y[k] for k in range(NY)]))
+    r.stat_z[0] = merged([r.stat_y[k] for k in range(NY)])
     copies = [
         send(r.stat_z.at[0], r.stat_z.at[d], r.sz, d, along_z(d)) for d in far_first(NZ)
     ]
     attention_backward(2)
     wait_all(copies)
-    policy_lognorm, frozen_lognorm, cross_total = merged([r.stat_z[k] for k in range(NZ)])
+    stats = merged([r.stat_z[k] for k in range(NZ)])
+    policy_lognorm, frozen_lognorm, cross_total = [unfold(stats, k) for k in range(3)]
 
     divergence = cross_total - policy_lognorm + frozen_lognorm
     policy_prob = jnp.exp(policy_logits - policy_lognorm)
@@ -604,7 +607,7 @@
         pl.when(c != half)(lambda half=half: product(half))
     part_rows = PART * SLOTS
     low_part, high_part = slice(0, part_rows), slice(part_rows, 2 * part_rows)
-    cores, reduced, copies_y, copies_z = [[], []], [[], []], [[], []], [[], []]
+    cores, reduced, copies_y = [[], []], [[], []], [[], []]
     for k in range(2):
         for i, group in enumerate([far, right, left, x]):
             r.outgoing[k, group] = r.total[2 * (1 - c) + k, group].astype(bf16)
@@ -676,19 +679,63 @@
         summed = r.send_y[k, y].astype(f32)
         for d in range(1, NY):
             summed += r.from_y[k, d].astype(f32)
-        r.from_z[k, z] = summed.astype(bf16)
-        block = r.from_z.at[k, z]
-        for d in far_first(NZ):
-            copies_z[k].append(send(block, block, r.rz, NZ * k + d, along_z(d)))
-
-    def start_core(k):
-        wait_all(copies_z[k])
-        summed = r.from_z[k, 0].astype(f32)
+        for j in range(TILES):
+            owner = TILES * k + j
+            r.send_z[owner] = summed[:, j * 128 : (j + 1) * 128].astype(bf16)
+            pl.when(z != owner)(lambda owner=owner: to_owner(owner).start())
+            pl.when(z == owner)(lambda owner=owner: keep_own(owner))
+
+    def to_owner(owner):
+        return pltpu.make_async_remote_copy(
+            src_ref=r.send_z.at[owner],
+            dst_ref=r.from_z.at[z],
+            send_sem=r.rz.at[0, owner],
+            recv_sem=r.rz.at[1, z],
+            device_id=device(x, y, owner, c),
+            device_id_type=MESH,
+        )
+
+    def keep_own(owner):
+        r.from_z[owner] = r.send_z[owner]
+
+    def arrival(block, sem):
+        return pltpu.make_async_remote_copy(
+            src_ref=block,
+            dst_ref=block,
+            send_sem=r.fc.at[0, 0],
+            recv_sem=sem,
+            device_id=across,
+            device_id_type=MESH,
+        )
+
+    column_peers = [(d, o) for d in far_first(NZ) for o in range(NC)] + [(0, 1)]
+
+    def to_column(k):
+        d, o = column_peers[k]
+        block = r.final.at[c, z]
+        return pltpu.make_async_remote_copy(
+            src_ref=block,
+            dst_ref=block,
+            send_sem=r.fc.at[0, k],
+            recv_sem=r.fc.at[1, c * NZ + z],
+            device_id=device(x, y, wrap(z + d, NZ), 1 - c if o else c),
+            device_id_type=MESH,
+        )
+
+    def sum_column():
         for d in range(1, NZ):
-            summed += r.from_z[k, d].astype(f32)
-        r.final[2 * c + k] = summed
-        block = r.final.at[2 * c + k]
-        return send(block, block, r.fc, k, across)
+            source = wrap(z + d, NZ)
+            arrival(r.from_z.at[source], r.rz.at[1, source]).wait_recv()
+        summed = r.from_z[0].astype(f32)
+        for k in range(1, NZ):
+            summed += r.from_z[k].astype(f32)
+        r.final[c, z] = summed.astype(bf16)
+        for k in range(len(column_peers)):
+            to_column(k).start()
+
+    def end_column():
+        for k in range(len(column_peers)):
+            to_column(k).wait_send()
 
     start_far(0)
     start_direct(0)
@@ -702,18 +749,26 @@
     start_z(0)
     start_z(1)
     load_proj.wait()
-    finals = [start_core(0), start_core(1)]
+    pl.when(z < 2 * TILES)(sum_column)
+    for core in range(NC):
+        for owner in range(2 * TILES):
+            block, sem = r.final.at[core, owner], r.fc.at[1, core * NZ + owner]
+            pl.when((c != core) | (z != owner))(
+                lambda block=block, sem=sem: arrival(block, sem).wait_recv()
+            )
     slot_grad = 0.0
-    for k in range(2):
-        finals[k].wait()
-        for q in (k, 2 + k):
-            stop = quarter_stop(q)
-            part = jnp.concatenate([r.final[q, :SLOTS, :], r.final[q, SLOTS:, :]], axis=1)
-            part = part[:, : stop - q * QUARTER]
-            r.hidden_grad[:, q * QUARTER : stop] = part
-            slot_grad += jnp.dot(
-                part.astype(bf16), r.proj[q * QUARTER : stop, :], preferred_element_type=f32
-            )
+    for q in range(4):
+        stop = quarter_stop(q)
+        tiles_of = [r.final[q // 2, TILES * (q % 2) + j].astype(f32) for j in range(TILES)]
+        pieces = [tile[:SLOTS] for tile in tiles_of] + [tile[SLOTS:] for tile in tiles_of]
+        part = jnp.concatenate(pieces, axis=1)[:, : stop - q * QUARTER]
+        r.hidden_grad[:, q * QUARTER : stop] = part
+        slot_grad += jnp.dot(
+            part.astype(bf16), r.proj[q * QUARTER : stop, :], preferred_element_type=f32
+        )
+    pl.when(z < 2 * TILES)(end_column)
+    for owner in range(2 * TILES):
+        pl.when(z != owner)(lambda owner=owner: to_owner(owner).wait_send())
     for copy in cores[0] + cores[1] + reduced[0] + reduced[1]:
         copy.wait_send()
     stores = []

time: 82.1 us -> 85.6 us (1.043)
  Pallas kernels: 81.3 us -> 84.5 us
    pallas_call x1, Pallas kernels: 79.5 us -> 82.7 us  [shards(): pl.pallas_call(kernel_of(names), out_shape=shapes, in_specs=[hbm] * len(o...]
where the time goes in v6:
time: 85.6 us; the launch traced here: 85.1 us
  Pallas kernels  84.5 us (99%)
    pallas_call x1, Pallas kernels, shards(): pl.pallas_call(kernel_of(names), out_shape=shapes, in_specs=[hbm] * len(o...  82.7 us
    pallas_call x1, Pallas kernels, shards(): pl.pallas_call(hand_over, out_shape=shapes, in_specs=[spec for _, _, spec...  1.78 us

profile of v6, /device:TPU:1, one launch (start us, length us, event | category | flops | bytes accessed | tf_op | source)
XLA Modules:
  0.0 85.1 jit_solution(7249155166719583921)
XLA Ops:
  0.6 82.7 %shard_map.165 = (bf16[512,256]{1,0:T(8,128)(2,1)}, bf16[2,32,512]{2,1,0:T(8,128)(2,1)}, f32[8,2880]{1,0:T(8,128)}, f32[4]{0:T(128)}) custom-call(bf16[8,2880]{1,0:T(8,128)(2,1)} %refs_0_.1, bf16[1,8]{1,0:T(2,128)(2,1)} %bitcast.5, s32[8]{0:T(128)} %refs_2_.1, s32[8]{0:T(128)} %refs_3_.1, s32[8]{0:T(128)} %refs_4_.1, f32[4]{0:T(128)} %refs_5_.1, ...), custom_call_target="tpu_custom_call" | custom-call | tf_op jit(solution)/shard_map/pallas_call | solution.py:912
  83.3 1.8 %shard_map.166 = (bf16[512,256]{1,0:T(8,128)(2,1)}, bf16[2,32,512]{2,1,0:T(8,128)(2,1)}, f32[8,2880]{1,0:T(8,128)}, f32[4]{0:T(128)}) custom-call(bf16[512,256]{1,0:T(8,128)(2,1)} %get-tuple-element.12.refs_0_, bf16[2,32,512]{2,1,0:T(8,128)(2,1)} %get-tuple-element.13.refs_1_, f32[8,2880]{1,0:T(8,128)} %get-tuple-element.14.refs_2_, f32[4]{0:T(128)} %get-tuple-element.15.refs_3_), custom_call_target="tpu_custom_call" | custom-call | tf_op jit(solution)/shard_map/pallas_call | solution.py:922

commit v7 on v5

--- a/solution.py
+++ b/solution.py
@@ -44,18 +44,18 @@
 
 
 def merged(blocks):
-    rows = [[unfold(block, k) for block in blocks] for k in range(3)]
-    tops = [rows[0][0], rows[1][0]]
-    for k in range(2):
-        for row in rows[k][1:]:
-            tops[k] = jnp.maximum(tops[k], row)
-    mass, cross, frozen = 0.0, 0.0, 0.0
-    for policy, other, mean in zip(*rows):
-        share = jnp.exp(policy - tops[0])
+    top = blocks[0]
+    for block in blocks[1:]:
+        top = jnp.maximum(top, block)
+    mass, cross = 0.0, 0.0
+    for block in blocks:
+        share = jnp.exp(block - top)
         mass += share
-        cross += share * mean
-        frozen += jnp.exp(other - tops[1])
-    return [tops[0] + jnp.log(mass), tops[1] + jnp.log(frozen), cross / mass]
+        cross += pltpu.roll(share, 2, axis=0) * block
+    row = lax.broadcasted_iota(jnp.int32, top.shape, 0)
+    return jnp.where(
+        (row == 2) | (row == 5), cross / pltpu.roll(mass, 2, axis=0), top + jnp.log(mass)
+    )
 
 
 def far_first(size):
@@ -218,8 +218,8 @@
             copy.wait()
 
     barrier = pltpu.get_barrier_semaphore()
-    peers = [along_x(d, o) for d, o in xc_steps]
-    peers += [along_y(d) for d in range(1, NY)] + [along_z(d) for d in range(1, NZ)]
+    peers = [along_y(d) for d in far_first(NY)] + [along_x(d, o) for d, o in xc_steps]
+    peers += [along_z(d) for d in far_first(NZ)]
     peers += [(owner, z * NC + o) for owner in (prev, after) for o in range(NC)]
     for peer in peers:
         pl.semaphore_signal(barrier, inc=1, device_id=peer, device_id_type=MESH)
@@ -555,21 +555,19 @@
         send(r.stat_xc.at[0], r.stat_xc.at[k + 1], r.sxc, k, along_x(d, o))
         for k, (d, o) in enumerate(xc_steps)
     ]
-    attention_backward(0)
     wait_all(copies)
-    r.stat_y[0] = fold(merged([r.stat_xc[k] for k in range(NX * NC)]))
+    r.stat_y[0] = merged([r.stat_xc[k] for k in range(NX * NC)])
     copies = [
         send(r.stat_y.at[0], r.stat_y.at[d], r.sy, d, along_y(d)) for d in far_first(NY)
     ]
-    attention_backward(1)
     wait_all(copies)
-    r.stat_z[0] = fold(merged([r.stat_y[k] for k in range(NY)]))
+    r.stat_z[0] = merged([r.stat_y[k] for k in range(NY)])
     copies = [
         send(r.stat_z.at[0], r.stat_z.at[d], r.sz, d, along_z(d)) for d in far_first(NZ)
     ]
-    attention_backward(2)
     wait_all(copies)
-    policy_lognorm, frozen_lognorm, cross_total = merged([r.stat_z[k] for k in range(NZ)])
+    stats = merged([r.stat_z[k] for k in range(NZ)])
+    policy_lognorm, frozen_lognorm, cross_total = [unfold(stats, k) for k in range(3)]
 
     divergence = cross_total - policy_lognorm + frozen_lognorm
     policy_prob = jnp.exp(policy_logits - policy_lognorm)
@@ -614,8 +612,6 @@
 
     for half in range(2):
         pl.when(c == half)(lambda half=half: product(half))
-    for t in range(3, tiles):
-        attention_backward(t)
 
     def pass_on(k, src, dst, target):
         reduced[k].append(send(src, dst, r.rx, 6 * k + len(reduced[k]), target))
@@ -693,10 +689,15 @@
     start_far(0)
     start_direct(0)
     start_far(1)
+    attention_backward(0)
     start_summed(0)
     start_direct(1)
+    attention_backward(1)
     start_summed(1)
+    attention_backward(2)
     start_y(0)
+    for t in range(3, tiles):
+        attention_backward(t)
     start_y(1)
     slot_setup()
     start_z(0)

time: 82.1 us -> 81.7 us (level)
  no operation moved by 1% of the time
where the time goes in v7:
time: 81.7 us; the launch traced here: 81.6 us
  Pallas kernels  80.9 us (99%)
    pallas_call x1, Pallas kernels, shards(): pl.pallas_call(kernel_of(names), out_shape=shapes, in_specs=[hbm] * len(o...  79.2 us
    pallas_call x1, Pallas kernels, shards(): pl.pallas_call(hand_over, out_shape=shapes, in_specs=[spec for _, _, spec...  1.78 us

profile of v7, /device:TPU:1, one launch (start us, length us, event | category | flops | bytes accessed | tf_op | source)
XLA Modules:
  0.0 81.6 jit_solution(6087229078215028292)
XLA Ops:
  0.6 79.2 %shard_map.165 = (bf16[512,256]{1,0:T(8,128)(2,1)}, bf16[2,32,512]{2,1,0:T(8,128)(2,1)}, f32[8,2880]{1,0:T(8,128)}, f32[4]{0:T(128)}) custom-call(bf16[8,2880]{1,0:T(8,128)(2,1)} %refs_0_.1, bf16[1,8]{1,0:T(2,128)(2,1)} %bitcast.5, s32[8]{0:T(128)} %refs_2_.1, s32[8]{0:T(128)} %refs_3_.1, s32[8]{0:T(128)} %refs_4_.1, f32[4]{0:T(128)} %refs_5_.1, ...), custom_call_target="tpu_custom_call" | custom-call | tf_op jit(solution)/shard_map/pallas_call | solution.py:858
  79.8 1.8 %shard_map.166 = (bf16[512,256]{1,0:T(8,128)(2,1)}, bf16[2,32,512]{2,1,0:T(8,128)(2,1)}, f32[8,2880]{1,0:T(8,128)}, f32[4]{0:T(128)}) custom-call(bf16[512,256]{1,0:T(8,128)(2,1)} %get-tuple-element.12.refs_0_, bf16[2,32,512]{2,1,0:T(8,128)(2,1)} %get-tuple-element.13.refs_1_, f32[8,2880]{1,0:T(8,128)} %get-tuple-element.14.refs_2_, f32[4]{0:T(128)} %get-tuple-element.15.refs_3_), custom_call_target="tpu_custom_call" | custom-call | tf_op jit(solution)/shard_map/pallas_call | solution.py:868

commit v8 on v7

--- a/solution.py
+++ b/solution.py
@@ -102,7 +102,7 @@
         "sink_y": pltpu.VMEM((NY, 1, WINDOW), f32),
         "sink_x": pltpu.VMEM((NX, 1, WINDOW), f32),
         "wide": pltpu.VMEM((4, SLOTS, QUARTER), f32),
-        "gathered": pltpu.VMEM((2, 2, NX, 2, PART, 2 * SLOTS, CHUNK), bf16),
+        "gathered": pltpu.VMEM((1, 2, NX, 2, PART, 2 * SLOTS, QUARTER), bf16),
         "rows": pltpu.VMEM((4, rows, QUARTER), bf16),
         "meta_y": pltpu.VMEM((NY,) + stat, f32),
         "meta_x": pltpu.VMEM((NX,) + stat, f32),
@@ -253,8 +253,7 @@
     for q in range(4):
         r.wide[q, :, : quarter_stop(q) - q * QUARTER] = hidden[:, q * QUARTER : quarter_stop(q)]
     packed = jnp.concatenate([r.wide[2 * c], r.wide[2 * c + 1]], axis=0).astype(bf16)
-    for k in range(2):
-        r.gathered[k, c, x, y_part, y_sub] = packed[:, k * CHUNK : (k + 1) * CHUNK]
+    r.gathered[0, c, x, y_part, y_sub] = packed
     wait_all(small)
     stat = r.meta_y.shape[1:]
     field = lax.broadcasted_iota(jnp.int32, stat, 0)
@@ -271,8 +270,8 @@
     r.meta_y[y] = meta
     pl.semaphore_wait(barrier, len(peers))
 
-    copies_y = [[], []]
-    for k in range(2):
+    copies_y = [[]]
+    for k in range(1):
         own_slot = r.gathered.at[k, c, x, y_part, y_sub]
         for d in far_first(NY):
             copies_y[k].append(send(own_slot, own_slot, r.gy, k * NY + d, along_y(d)))
@@ -447,12 +446,12 @@
         order[k].append((group, part))
 
     def arrange(k, half, group, part):
-        block = r.gathered[k, half, group, part].astype(f32).reshape(PART, 2, SLOTS, CHUNK)
+        block = r.gathered[k, half, group, part].astype(f32).reshape(PART, 2, SLOTS, QUARTER)
         start = pl.multiple_of((group * 2 + part) * (PART * SLOTS), PART * SLOTS)
         for low in range(2):
-            r.rows[
-                2 * half + low, pl.ds(start, PART * SLOTS), k * CHUNK : (k + 1) * CHUNK
-            ] = block[:, low].reshape(PART * SLOTS, CHUNK).astype(bf16)
+            r.rows[2 * half + low, pl.ds(start, PART * SLOTS), :] = (
+                block[:, low].reshape(PART * SLOTS, QUARTER).astype(bf16)
+            )
 
     def spread(k):
         wait_all(copies_y[k])
@@ -495,20 +494,15 @@
     r.meta_x[x] = meta
     metas_x = [send(r.meta_x.at[x], r.meta_x.at[x], r.mx, d, along_x(d)) for d in range(1, NX)]
     attention_setup()
-    spread(1)
     relay_on(0)
     attention_forward(0)
-    relay_on(1)
     direct_rest(0)
     attention_forward(1)
-    direct_rest(1)
     far_rest(0)
     attention_forward(2)
     arrange_own(0)
-    far_rest(1)
     for t in range(3, tiles):
         attention_forward(t)
-    arrange_own(1)
     load_policy.wait()
     load_frozen.wait()
 
@@ -527,7 +521,7 @@
 
     for half in range(2):
         pl.when(c == half)(lambda half=half: add_logits(half, True))
-    for k in range(2):
+    for k in range(1):
         for copy, (group, part) in zip(sent_c[k], order[k]):
             copy.wait_recv()
             arrange(k, 1 - c, group, part)

time: 81.7 us -> 81.3 us (level)
  no operation moved by 1% of the time
where the time goes in v8:
time: 81.3 us; the launch traced here: 81.1 us
  Pallas kernels  80.4 us (99%)
    pallas_call x1, Pallas kernels, shards(): pl.pallas_call(kernel_of(names), out_shape=shapes, in_specs=[hbm] * len(o...  78.6 us
    pallas_call x1, Pallas kernels, shards(): pl.pallas_call(hand_over, out_shape=shapes, in_specs=[spec for _, _, spec...  1.78 us

profile of v8, /device:TPU:1, one launch (start us, length us, event | category | flops | bytes accessed | tf_op | source)
XLA Modules:
  0.0 81.1 jit_solution(13517630805993370169)
XLA Ops:
  0.6 78.6 %shard_map.165 = (bf16[512,256]{1,0:T(8,128)(2,1)}, bf16[2,32,512]{2,1,0:T(8,128)(2,1)}, f32[8,2880]{1,0:T(8,128)}, f32[4]{0:T(128)}) custom-call(bf16[8,2880]{1,0:T(8,128)(2,1)} %refs_0_.1, bf16[1,8]{1,0:T(2,128)(2,1)} %bitcast.5, s32[8]{0:T(128)} %refs_2_.1, s32[8]{0:T(128)} %refs_3_.1, s32[8]{0:T(128)} %refs_4_.1, f32[4]{0:T(128)} %refs_5_.1, ...), custom_call_target="tpu_custom_call" | custom-call | tf_op jit(solution)/shard_map/pallas_call | solution.py:852
  79.3 1.8 %shard_map.166 = (bf16[512,256]{1,0:T(8,128)(2,1)}, bf16[2,32,512]{2,1,0:T(8,128)(2,1)}, f32[8,2880]{1,0:T(8,128)}, f32[4]{0:T(128)}) custom-call(bf16[512,256]{1,0:T(8,128)(2,1)} %get-tuple-element.12.refs_0_, bf16[2,32,512]{2,1,0:T(8,128)(2,1)} %get-tuple-element.13.refs_1_, f32[8,2880]{1,0:T(8,128)} %get-tuple-element.14.refs_2_, f32[4]{0:T(128)} %get-tuple-element.15.refs_3_), custom_call_target="tpu_custom_call" | custom-call | tf_op jit(solution)/shard_map/pallas_call | solution.py:862
